TPU v7x, 256 devices: a whole 4x4x8 slice. The times are simulated.
256 devices in a mesh: bg: 4 (over z_hi), pw: 64 (over y, z_lo, x, core).
Axes of the slice: x: 4, y: 4, z: 8 (z_hi: 4, z_lo: 2; z = z_hi * 2 + z_lo), core: 2. Of those that a mesh axis runs over, the one named last changes fastest.
Arguments:
- orbitals: float32 [8, 4096, 256], P('bg', 'pw'), may hold values from -6 to 6
- applied_orbitals: float32 [8, 4096, 256], P('bg', 'pw'), may hold values from -6 to 6
- potential: float32 [320, 320, 320], P('pw'), may hold values from -6 to 6
- stick_map: int32 [4096], replicated, may hold values from 0 to 16383, as said below
- ritz_values: float32 [8], P('bg'), may hold values from -1 to 1
- ritz_rotation: float32 [16, 8], replicated, may hold values from -1.5 to 1.5
Outputs:
- next_orbitals: float32 [8, 4096, 256], P('bg', 'pw')
- applied_correction: float32 [8, 4096, 256], P('bg', 'pw')
Inputs may be any that keep to these rules, and one draw needn't show every extreme that they name: `stick_map`: the 4096 values are distinct.
All inputs are finite; a program needn't handle non-finite values.
Results may differ from a plain program's by a relative error of at most 0.00007.
Values sent between devices are 32-bit elements; how exact they have to be, the bound alone decides.
No kernel may reach another device: no remote copies, remote signals or barrier semaphores. Data moves between devices by JAX's collectives and lax.ppermute only.
A program may use at most 64 MiB of HBM per device.

v0:
```python
import functools
import math

import jax
import jax.numpy as jnp
import ml_dtypes
import numpy as np
from jax import lax
from jax.experimental import pallas as pl
from jax.experimental.pallas import tpu as pltpu
from jax.sharding import PartitionSpec as P

F32 = jnp.float32
BF16 = jnp.bfloat16
VMEM = pl.BlockSpec(memory_space=pltpu.VMEM)
SMEM = pl.BlockSpec(memory_space=pltpu.SMEM)
PARAMS = pltpu.CompilerParams(vmem_limit_bytes=56 * 1024 * 1024)

LENGTH = 320
WIDTH = 128
FINE = 2 * WIDTH
GROUP = 64
PLANES = LENGTH // GROUP
PARTS = 2 * PLANES
STICKS = GROUP * 64
BANDS = 2


def split_host(table):
    high = table.astype(ml_dtypes.bfloat16)
    low = (table - high.astype(np.float64)).astype(ml_dtypes.bfloat16)
    return high, low


def complex_table(length):
    frequencies = np.arange(WIDTH) - WIDTH // 2
    angles = 2.0 * math.pi * (np.outer(frequencies, np.arange(length)) % length) / length
    cosine, sine = np.cos(angles) / math.sqrt(length), np.sin(angles) / math.sqrt(length)
    return np.concatenate(
        [np.concatenate([cosine, sine], 1), np.concatenate([-sine, cosine], 1)], 0
    )


def resampling_table():
    places = np.arange(FINE)[:, None] * LENGTH - np.arange(LENGTH)[None, :] * FINE
    total = np.zeros((FINE, LENGTH))
    for d in range(-(WIDTH - 1), WIDTH):
        total += np.cos(2.0 * math.pi * ((places * d) % (FINE * LENGTH)) / (FINE * LENGTH))
    return total / LENGTH


def tables():
    square = complex_table(FINE)
    high, low = split_host(square)
    stick = complex_table(LENGTH).reshape(2 * WIDTH, 2, GROUP, PLANES)
    stick = stick.transpose(0, 2, 1, 3).reshape(2 * WIDTH, GROUP * PARTS)
    s_high, s_low = split_host(stick)
    r_high, r_low = split_host(resampling_table())
    three = np.concatenate
    return dict(
        row_up=three([high, high, low], 0),
        row_down=three([high.T, high.T, low.T], 0),
        col_up=three([high.T, low.T, high.T], 1),
        col_down=three([high, low, high], 1),
        stick_up=three([s_high.T, s_low.T, s_high.T], 1),
        stick_down=three([s_high, s_low, s_high], 1),
        fine_cols=three([r_high, r_low, r_high], 1),
        fine_rows=np.stack([r_high.T, r_low.T]),
    )


def halves(x):
    high = x.astype(BF16)
    low = (x - high.astype(F32)).astype(BF16)
    return high, low


def data_rows(x, axis):
    high, low = halves(x)
    return jnp.concatenate([high, high, low] if axis == 0 else [high, low, high], axis)


def dot(a, b):
    return jnp.dot(a, b, preferred_element_type=F32)


def planar_of(map_ref, sticks):
    me = lax.axis_index("pw")
    per_row = 128 // sticks
    row = map_ref[pl.ds(me // per_row, 1), :]
    fx = (row >> 7) - WIDTH // 2
    fy = (row & (WIDTH - 1)) - WIDTH // 2
    planar = (fx * fx + fy * fy).astype(F32)
    turned = jnp.broadcast_to(planar, (128, 128)).T
    upper = lax.rem(me, per_row) == 1
    return jnp.where(upper, turned[sticks:], turned[:sticks])


def kinetic_of(map_ref, sticks):
    planar = planar_of(map_ref, sticks)
    fz = lax.broadcasted_iota(jnp.int32, (1, WIDTH), 1) - WIDTH // 2
    return (planar + (fz * fz).astype(F32)) * (1.0 / (WIDTH // 2) ** 2)


def before_kernel(values_ref, rotation_ref, map_ref, orb_ref, app_ref, up_ref, send_ref, corr_ref, mix_ref):
    sticks = orb_ref.shape[1]
    kinetic = kinetic_of(map_ref, sticks)
    scale = 1.0 + jnp.concatenate([kinetic, kinetic], 1)
    corr = []
    for b in range(BANDS):
        c = (app_ref[b] - values_ref[b] * orb_ref[b]) / scale
        corr_ref[b] = c
        corr.append(c)
    rows = jnp.concatenate(corr, 0)
    turned = jnp.concatenate([rows[:, :128].T, rows[:, 128:].T], 0)
    send_ref[...] = dot(up_ref[...], data_rows(turned, 0))
    first = lax.axis_index("bg") * BANDS
    all_bands = mix_ref.shape[0]
    for j in range(all_bands):
        total = None
        for b in range(BANDS):
            term = rotation_ref[first + b, j] * orb_ref[b]
            term = term + rotation_ref[all_bands + first + b, j] * corr[b]
            total = term if total is None else total + term
        mix_ref[j] = total


def potential_kernel(pot_ref, rows_ref, cols_ref, out_ref, work):
    rows_high, rows_low = rows_ref[0], rows_ref[1]
    for p in range(PLANES):
        high, low = halves(pot_ref[p])
        part = dot(high, rows_high) + (dot(low, rows_high) + dot(high, rows_low))
        work[...] = data_rows(part, 0)
        out_ref[p] = dot(cols_ref[...], work[...])


def middle_kernel(
    place_ref, recv_ref, pot_ref, row_up, col_up, col_down, row_down, send_ref,
    sticks_ref, square_ref, turned_ref, rows_ref, half_ref, back_ref, out_ref,
):
    lane = lax.broadcasted_iota(jnp.int32, (1, 128), 1)
    lane_block = lane >> 5
    second_band = ((lane >> 4) & 1) == 1

    def unpack(d, _):
        real = recv_ref[pl.ds(d * PARTS, 8), :]
        imag = recv_ref[pl.ds(d * PARTS + 2, 8), :]
        turned = jnp.concatenate([real, imag] * 8, 0).T
        sticks_ref[pl.ds(pl.multiple_of(d * 64, 64), 64), :] = jnp.where(second_band, turned[64:], turned[:64])
        return 0

    lax.fori_loop(0, GROUP, unpack, 0, unroll=4)
    square_ref[...] = jnp.zeros_like(square_ref)

    def scatter(i, _):
        for j in range(16):
            s = i * 16 + j
            place = place_ref[s]
            pltpu.store(
                square_ref.at[pl.ds(place >> 2, 1), :],
                sticks_ref[pl.ds(s, 1), :],
                mask=lane_block == (place & 3),
            )
        return 0

    lax.fori_loop(0, STICKS // 16, scatter, 0)

    def turn(i, _):
        rows = pl.ds(pl.multiple_of(i * 128, 128), 128)
        turned_ref[rows, :] = square_ref[rows, :].T
        return 0

    lax.fori_loop(0, 32, turn, 0, unroll=4)
    for b in range(BANDS):
        for p in range(PLANES):
            at = (b * PLANES + p) * 128
            real = turned_ref[pl.ds(b * 16 + p, 128, stride=32), :]
            imag = turned_ref[pl.ds(b * 16 + 8 + 3 + p, 128, stride=32), :]
            rows_ref[at : at + 128, : 6 * 128] = data_rows(jnp.concatenate([real, imag], 1), 1)
    half_ref[...] = dot(rows_ref[:, : 6 * 128], row_up[...])
    for b in range(BANDS):
        for p in range(PLANES):
            at = (b * PLANES + p) * 128
            part = half_ref[at : at + 128, :]
            part = jnp.concatenate([part[:, :FINE], part[:, FINE:]], 0)
            field = dot(col_up[...], data_rows(part, 0))
            local = pot_ref[p]
            product = field * jnp.concatenate([local, local], 0)
            part = dot(col_down[...], data_rows(product, 0))
            part = jnp.concatenate([part[:128], part[128:]], 1)
            rows_ref[at : at + 128, :] = data_rows(part, 1)
    back_ref[...] = dot(rows_ref[...], row_down[...])
    for b in range(BANDS):
        for p in range(PLANES):
            at = (b * PLANES + p) * 128
            for c in range(2):
                turned_ref[pl.ds(b * 16 + c * 8 + p, 128, stride=32), :] = back_ref[
                    at : at + 128, c * 128 : c * 128 + 128
                ]

    def turn_back(i, _):
        rows = pl.ds(pl.multiple_of(i * 128, 128), 128)
        square_ref[rows, :] = turned_ref[rows, :].T
        return 0

    lax.fori_loop(0, 32, turn_back, 0, unroll=4)

    def gather(i, _):
        for j in range(16):
            s = i * 16 + j
            place = place_ref[s]
            row = square_ref[pl.ds(place >> 2, 1), :]
            sticks_ref[pl.ds(s, 1), :] = jnp.where(lane_block == (place & 3), row, 0.0)
        return 0

    lax.fori_loop(0, STICKS // 16, gather, 0)

    def pack(d, _):
        rows = sticks_ref[pl.ds(pl.multiple_of(d * 64, 64), 64), :]
        upper = jnp.where(second_band, 0.0, rows)
        lower = jnp.where(second_band, rows, 0.0)
        turned = jnp.concatenate([upper, lower], 0).T
        total = turned[:16]
        for k in range(1, 8):
            total = total + turned[16 * k : 16 * k + 16]
        out_ref[pl.ds(d * PARTS, PLANES), :] = total[:PLANES]
        out_ref[pl.ds(d * PARTS + PLANES, PLANES), :] = total[8 : 8 + PLANES]
        return 0

    lax.fori_loop(0, GROUP, pack, 0, unroll=4)
    send_ref[...] = out_ref[...]


def after_kernel(map_ref, corr_ref, recv_ref, down_ref, out_ref):
    sticks = corr_ref.shape[1]
    kinetic = kinetic_of(map_ref, sticks)
    local = dot(down_ref[...], data_rows(recv_ref[...], 0))
    local = jnp.concatenate([local[:128].T, local[128:].T], 1)
    both = jnp.concatenate([kinetic, kinetic], 1)
    for b in range(BANDS):
        out_ref[b] = both * corr_ref[b] + local[b * sticks : (b + 1) * sticks]


def shape(*dims):
    return jax.ShapeDtypeStruct(dims, F32)


def exchange(values):
    values = values.reshape(GROUP, 1, PARTS * 128)
    return lax.all_to_all(values, "pw", 0, 0, tiled=True).reshape(GROUP * PARTS, 128)


def middle(place, received, local, t):
    return pl.pallas_call(
        middle_kernel,
        out_shape=shape(GROUP * PARTS, 128),
        in_specs=[SMEM] + [VMEM] * 6,
        out_specs=VMEM,
        scratch_shapes=[
            pltpu.VMEM((STICKS, 128), F32),
            pltpu.VMEM((STICKS, 128), F32),
            pltpu.VMEM((STICKS, 128), F32),
            pltpu.VMEM((BANDS * PLANES * 128, 6 * FINE), BF16),
            pltpu.VMEM((BANDS * PLANES * 128, 2 * FINE), F32),
            pltpu.VMEM((BANDS * PLANES * 128, FINE), F32),
            pltpu.VMEM((GROUP * PARTS, 128), F32),
        ],
        compiler_params=PARAMS,
        name="middle",
    )(place, received, local, t["row_up"], t["col_up"], t["col_down"], t["row_down"])


def fine_potential(potential, t):
    return pl.pallas_call(
        potential_kernel,
        out_shape=shape(PLANES, FINE, FINE),
        in_specs=[VMEM] * 3,
        out_specs=VMEM,
        scratch_shapes=[pltpu.VMEM((3 * LENGTH, FINE), BF16)],
        compiler_params=PARAMS,
        name="fine_potential",
    )(potential, t["fine_rows"], t["fine_cols"])


def on_device(orbitals, applied_orbitals, potential, stick_map, ritz_values, ritz_rotation):
    t = {name: jnp.asarray(value) for name, value in tables().items()}
    sticks = orbitals.shape[1]
    all_bands = ritz_rotation.shape[1]
    map_rows = stick_map.reshape(-1, 128)
    place = ((stick_map >> 9) << 9) | ((stick_map & 127) << 2) | ((stick_map >> 7) & 3)
    sent, correction, mixed = pl.pallas_call(
        before_kernel,
        out_shape=(shape(GROUP * PARTS, 128), shape(*orbitals.shape), shape(all_bands, sticks, 2 * WIDTH)),
        in_specs=[SMEM, SMEM] + [VMEM] * 4,
        out_specs=(VMEM, VMEM, VMEM),
        compiler_params=PARAMS,
        name="before",
    )(ritz_values, ritz_rotation, map_rows, orbitals, applied_orbitals, t["stick_up"])
    local = fine_potential(potential, t)
    next_orbitals = lax.psum_scatter(mixed, "bg", scatter_dimension=0, tiled=True)
    received = exchange(sent)
    returned = exchange(middle(place, received, local, t))
    applied_correction = pl.pallas_call(
        after_kernel,
        out_shape=shape(*orbitals.shape),
        in_specs=[VMEM] * 4,
        out_specs=VMEM,
        compiler_params=PARAMS,
        name="after",
    )(map_rows, correction, returned, t["stick_down"])
    return (next_orbitals, applied_correction)


def solution(mesh):
    return jax.shard_map(
        on_device,
        mesh=mesh,
        in_specs=(P("bg", "pw", None), P("bg", "pw", None), P("pw", None, None), P(), P("bg"), P()),
        out_specs=(P("bg", "pw", None), P("bg", "pw", None)),
        check_vma=False,
    )
```

profile of v0, /device:TPU:1, one launch (start us, length us, event | category | flops | bytes accessed | tf_op | source)
XLA Modules:
  0.0 92.7 jit_solution(9169706486414898441)
XLA Ops:
  7.2 1.4 %copy.17.rotation_ref = f32[16,8]{1,0:T(8,128)} copy(f32[16,8]{0,1:T(8,128)} %param.19) | data formatting | bytes 1024 | tf_op args[5]
  8.5 2.8 %before.1 = (f32[640,128]{1,0:T(8,128)}, f32[2,64,256]{2,1,0:T(8,128)}, f32[8,64,256]{2,1,0:T(8,128)}) custom-call(f32[2]{0:T(128)} %values_ref.1, f32[16,8]{1,0:T(8,128)} %copy.17.rotation_ref, s32[32,128]{1,0:T(8,128)} %bitcast.9, f32[2,64,256]{2,1,0:T(8,128)} %orb_ref.1, f32[2,64,256]{2,1,0:T(8,128)} %app_ref.1, bf16[640,768]{1,0:T(8,128)(2,1)} %constant.30.clone.up_ref), custom_call_target="tpu_custom_call" | custom-call | tf_op jit(solution)/shard_map/before/pallas_call | solution.py:291
  11.3 10.3 %all-to-all-start = ((f32[64,1,1280]{2,1,0:T(1,128)}), f32[64,1,1280]{2,1,0:T(1,128)S(1)}, u32[]{:S(2)}, u32[]{:S(2)}) async-start(f32[64,1,1280]{2,1,0:T(1,128)} %bitcast.8), calls=%async_computation.1 | async-start | bytes 655360 | tf_op jit(solution)/shard_map/all_to_all | solution.py:250
  21.7 0.0 reduce-scatter.2.cloned.1.call-start
  21.7 0.0 copy-start.1
  21.8 0.7 reduce-scatter.2.cloned.1.call-update
  22.4 7.3 %fine_potential.1.pot_ref = f32[5,256,256]{2,1,0:T(8,128)} custom-call(f32[5,320,320]{2,1,0:T(8,128)} %pot_ref.1, bf16[2,320,256]{2,1,0:T(8,128)(2,1)} %constant.33.clone.rows_ref, bf16[256,960]{1,0:T(8,128)(2,1)} %constant.32.clone.cols_ref), custom_call_target="tpu_custom_call" | custom-call | tf_op jit(solution)/shard_map/fine_potential/pallas_call | solution.py:274
  29.8 0.0 copy-done.1
  29.8 0.6 and_or_fusion.place_ref
  30.4 1.8 %all-to-all-done = f32[64,1,1280]{2,1,0:T(1,128)S(1)} async-done(((f32[64,1,1280]{2,1,0:T(1,128)}), f32[64,1,1280]{2,1,0:T(1,128)S(1)}, u32[]{:S(2)}, u32[]{:S(2)}) %all-to-all-start) | async-done | bytes 327712 | tf_op jit(solution)/shard_map/all_to_all | solution.py:250
  32.2 0.0 copy-start
  32.2 0.7 copy-done
  32.9 32.8 %middle.1 = f32[640,128]{1,0:T(8,128)} custom-call(s32[4096]{0:T(1024)} %and_or_fusion.place_ref, f32[640,128]{1,0:T(8,128)} %bitcast.5, f32[5,256,256]{2,1,0:T(8,128)} %fine_potential.1.pot_ref, bf16[768,512]{1,0:T(8,128)(2,1)} %constant.26.clone.row_up, bf16[512,768]{1,0:T(8,128)(2,1)} %constant.28.clone.col_up, ...), custom_call_target="tpu_custom_call" | custom-call | tf_op jit(solution)/shard_map/middle/pallas_call | solution.py:254
  65.7 17.7 %all_to_all.10 = f32[64,1,1280]{2,1,0:T(1,128)} all-to-all(f32[64,1,1280]{2,1,0:T(1,128)} %bitcast.6), channel_id=1, replica_groups=mesh['bg'=4,'pw'=64] {'pw'}, dimensions={0} | all-to-all | bytes 655360 | tf_op jit(solution)/shard_map/all_to_all | solution.py:250
  83.3 2.6 %after.1 = f32[2,64,256]{2,1,0:T(8,128)} custom-call(s32[32,128]{1,0:T(8,128)} %bitcast.10, f32[2,64,256]{2,1,0:T(8,128)} %get-tuple-element.6.corr_ref, f32[640,128]{1,0:T(8,128)} %bitcast.7, bf16[256,1920]{1,0:T(8,128)(2,1)} %constant.31.clone.down_ref), custom_call_target="tpu_custom_call" | custom-call | tf_op jit(solution)/shard_map/after/pallas_call | solution.py:303
  85.9 0.0 reduce-scatter.2.cloned.1.call-done
Async XLA Ops:
  11.3 20.8 %all-to-all-start = ((f32[64,1,1280]{2,1,0:T(1,128)}), f32[64,1,1280]{2,1,0:T(1,128)S(1)}, u32[]{:S(2)}, u32[]{:S(2)}) async-start(f32[64,1,1280]{2,1,0:T(1,128)} %bitcast.8), calls=%async_computation.1 | async-start | bytes 655360 | tf_op jit(solution)/shard_map/all_to_all | solution.py:250
  21.7 64.2 %reduce-scatter.2.cloned.1.call-start = ((), (), s32[]{:S(2)}) async-start(), calls=%async_computation.3 | async-start | bytes 655360 | tf_op jit(solution)/shard_map/reduce_scatter | solution.py:300
  21.7 8.0 %copy-start.1 = (s32[4096]{0:T(1024)S(1)}, s32[4096]{0:T(1024)}, u32[]{:S(2)}) copy-start(s32[4096]{0:T(1024)} %param.17) | copy-start | bytes 49156
  32.2 0.7 copy-start
Sparse Core Ops, SparseCore 0:
  25.6 28.5 reduce-scatter.1
where the time goes:
time: 93.1 us; the launch traced here: 92.7 us
  Pallas kernels  45.5 us (49%)
  blocking collectives  17.7 us (19%)
  between operations  14 us (15%)
  starting transfers between devices  10.4 us (11%)
  waiting for transfers between devices  2.44 us (3%)
  local copies, waits for them, and re-layouts  2.08 us (2%)
    pallas_call x1, Pallas kernels, middle(): pl.pallas_call(middle_kernel, out_shape=shape(GROUP * PARTS, 128), in_spe...  32.8 us
    all_to_all x1, blocking collectives, exchange(): lax.all_to_all(values, 'pw', 0, 0, tiled=True).reshape(GROUP * PARTS, 128)  17.7 us
    all_to_all x1, starting transfers between devices, exchange(): lax.all_to_all(values, 'pw', 0, 0, tiled=True).reshape(GROUP * PARTS, 128)  10.3 us
    pallas_call x1, Pallas kernels, fine_potential(): pl.pallas_call(potential_kernel, out_shape=shape(PLANES, FINE, FINE), in_...  7.34 us
    pallas_call x1, Pallas kernels, on_device(): pl.pallas_call(before_kernel, out_shape=(shape(GROUP * PARTS, 128), shape...  2.82 us
    pallas_call x1, Pallas kernels, on_device(): pl.pallas_call(after_kernel, out_shape=shape(*orbitals.shape), in_specs=[...  2.55 us
    unnamed x5, local copies, waits for them, and re-layouts  2.08 us
  transfers between devices with their start and end apart: 2, of which 1 were waited for; matrix products, arithmetic and copies ran while one was open for 1% of the time, Pallas kernels for 46%

commit v1 on v0

v1 whole, which is shorter than its diff:
```python
import functools
import math

import jax
import jax.numpy as jnp
import ml_dtypes
import numpy as np
from jax import lax
from jax.experimental import pallas as pl
from jax.experimental.pallas import tpu as pltpu
from jax.sharding import PartitionSpec as P

F32 = jnp.float32
BF16 = jnp.bfloat16
VMEM = pl.BlockSpec(memory_space=pltpu.VMEM)
SMEM = pl.BlockSpec(memory_space=pltpu.SMEM)
ANY = pl.BlockSpec(memory_space=pl.ANY)
PARAMS = pltpu.CompilerParams(vmem_limit_bytes=40 * 1024 * 1024)

LENGTH = 320
WIDTH = 128
FINE = 2 * WIDTH
GROUP = 64
PLANES = LENGTH // GROUP
PARTS = 2 * PLANES
STICKS = GROUP * 64
BANDS = 2


def split_host(table):
    high = table.astype(ml_dtypes.bfloat16)
    low = (table - high.astype(np.float64)).astype(ml_dtypes.bfloat16)
    return high, low


def complex_table(length):
    frequencies = np.arange(WIDTH) - WIDTH // 2
    angles = 2.0 * math.pi * (np.outer(frequencies, np.arange(length)) % length) / length
    cosine, sine = np.cos(angles) / math.sqrt(length), np.sin(angles) / math.sqrt(length)
    return np.concatenate(
        [np.concatenate([cosine, sine], 1), np.concatenate([-sine, cosine], 1)], 0
    )


def resampling_table():
    places = np.arange(FINE)[:, None] * LENGTH - np.arange(LENGTH)[None, :] * FINE
    total = np.zeros((FINE, LENGTH))
    for d in range(-(WIDTH - 1), WIDTH):
        total += np.cos(2.0 * math.pi * ((places * d) % (FINE * LENGTH)) / (FINE * LENGTH))
    return total / LENGTH


def spreading_table():
    table = np.zeros((2, 2, 8, 16, 8, 4, 2, 16))
    for b in range(2):
        for k in range(8):
            for part in range(16):
                table[b, :, k, part, k, :, b, part] = 1.0
    return table.reshape(512, 1024).astype(ml_dtypes.bfloat16)


def choosing_table():
    table = np.zeros((2, 16, 2, 4, 2, 16))
    for b in range(2):
        for part in range(16):
            table[b, part, :, :, b, part] = 1.0
    return table.reshape(32, 256).astype(ml_dtypes.bfloat16)


def tables():
    square = complex_table(FINE)
    high, low = split_host(square)
    stick = complex_table(LENGTH).reshape(2 * WIDTH, 2, GROUP, PLANES)
    stick = stick.transpose(0, 2, 1, 3).reshape(2 * WIDTH, GROUP * PARTS)
    s_high, s_low = split_host(stick)
    r_high, r_low = split_host(resampling_table())
    three = np.concatenate
    return dict(
        row_up=three([high, high, low], 0),
        row_down=three([high.T, high.T, low.T], 0),
        col_up=three([high.T, low.T, high.T], 1),
        col_down=three([high, low, high], 1),
        stick_up=three([s_high.T, s_low.T, s_high.T], 1),
        stick_down=three([s_high, s_low, s_high], 1),
        fine_cols=three([r_high, r_low, r_high], 1),
        spread=spreading_table(),
        choose=choosing_table(),
        fine_rows=np.stack([r_high.T, r_low.T]),
    )


def halves(x):
    high = x.astype(BF16)
    low = (x - high.astype(F32)).astype(BF16)
    return high, low


def data_rows(x, axis):
    high, low = halves(x)
    return jnp.concatenate([high, high, low] if axis == 0 else [high, low, high], axis)


def dot(a, b):
    return jnp.dot(a, b, preferred_element_type=F32)


def planar_of(map_ref, sticks):
    me = lax.axis_index("pw")
    per_row = 128 // sticks
    row = map_ref[pl.ds(me // per_row, 1), :]
    fx = (row >> 7) - WIDTH // 2
    fy = (row & (WIDTH - 1)) - WIDTH // 2
    planar = (fx * fx + fy * fy).astype(F32)
    turned = jnp.broadcast_to(planar, (128, 128)).T
    upper = lax.rem(me, per_row) == 1
    return jnp.where(upper, turned[sticks:], turned[:sticks])


def kinetic_of(map_ref, sticks):
    planar = planar_of(map_ref, sticks)
    fz = lax.broadcasted_iota(jnp.int32, (1, WIDTH), 1) - WIDTH // 2
    return (planar + (fz * fz).astype(F32)) * (1.0 / (WIDTH // 2) ** 2)


def before_kernel(values_ref, map_ref, orb_ref, app_ref, up_ref, send_ref, corr_ref):
    sticks = orb_ref.shape[1]
    kinetic = kinetic_of(map_ref, sticks)
    scale = 1.0 + jnp.concatenate([kinetic, kinetic], 1)
    corr = []
    for b in range(BANDS):
        c = (app_ref[b] - values_ref[b] * orb_ref[b]) / scale
        corr_ref[b] = c
        corr.append(c)
    rows = jnp.concatenate(corr, 0)
    turned = jnp.concatenate([rows[:, :128].T, rows[:, 128:].T], 0)
    send_ref[...] = dot(up_ref[...], data_rows(turned, 0))


def prepare_kernel(
    rotation_ref, map_ref, orb_ref, corr_ref, pot_hbm, rows_ref, cols_ref, out_ref, mask_ref, place_ref, keep_ref, pass_ref,
    pot_ref, work_ref, sems,
):
    copies = []
    for p in range(PLANES):
        copies.append(pltpu.make_async_copy(pot_hbm.at[p], pot_ref.at[p], sems.at[p]))
        copies[-1].start()
    me = lax.axis_index("bg")
    all_bands = rotation_ref.shape[0]
    for target, group in ((keep_ref, me), (pass_ref, me ^ 1)):
        for k, owner in enumerate((group, 3 - group)):
            for i in range(BANDS):
                j = owner * BANDS + i
                total = None
                for b in range(BANDS):
                    term = rotation_ref[j, me * BANDS + b] * orb_ref[b]
                    term = term + rotation_ref[j, all_bands + me * BANDS + b] * corr_ref[b]
                    total = term if total is None else total + term
                target[k, i] = total
    place_ref[...] = ((map_ref[...] >> 9) << 7) | (map_ref[...] & 127)
    lane_block = lax.broadcasted_iota(jnp.int32, (128, 128), 1) >> 5

    def mark(i, _):
        blocks = jnp.broadcast_to((map_ref[pl.ds(i, 1), :] >> 7) & 3, (128, 128)).T
        mask_ref[pl.ds(pl.multiple_of(i * 128, 128), 128), :] = jnp.where(blocks == lane_block, 1.0, 0.0)
        return 0

    lax.fori_loop(0, STICKS // 128, mark, 0, unroll=4)
    rows_high, rows_low = rows_ref[0], rows_ref[1]
    for p in range(PLANES):
        copies[p].wait()
        for at in range(0, LENGTH, LENGTH // 2):
            high, low = halves(pot_ref[p, at : at + LENGTH // 2, :])
            part = dot(high, rows_high) + (dot(low, rows_high) + dot(high, rows_low))
            high, low = halves(part)
            work_ref[p, at : at + LENGTH // 2] = high
            work_ref[p, LENGTH + at : LENGTH + at + LENGTH // 2] = high
            work_ref[p, 2 * LENGTH + at : 2 * LENGTH + at + LENGTH // 2] = low
        out_ref[p] = dot(cols_ref[...], work_ref[p])


def middle_kernel(
    place_hbm, recv_ref, pot_hbm, mask_ref, spread_hbm, row_up_hbm, col_up_hbm, col_down_hbm, row_down_hbm, choose_hbm,
    send_ref,
    place_ref, pot_ref, sticks_ref, square_ref, turned_ref, rows_ref, half_ref, back_ref,
    spread, row_up, col_up, col_down, row_down, choose, sems,
):
    copies = [
        pltpu.make_async_copy(source, target, sems.at[i])
        for i, (source, target) in enumerate(
            (
                (spread_hbm, spread),
                (place_hbm, place_ref),
                (row_up_hbm, row_up),
                (pot_hbm, pot_ref),
                (col_up_hbm, col_up),
                (col_down_hbm, col_down),
                (row_down_hbm, row_down),
                (choose_hbm, choose),
            )
        )
    ]
    for copy in copies:
        copy.start()
    square_ref[...] = jnp.zeros_like(square_ref)
    lane = lax.broadcasted_iota(jnp.int32, (1, 128), 1)

    for g in range(GROUP // 8):
        parts = []
        for d in range(8 * g, 8 * g + 8):
            parts += [recv_ref[d * PARTS : d * PARTS + 8, :], recv_ref[d * PARTS + 2 : d * PARTS + 10, :]]
        turned = jnp.concatenate(parts, 0).T
        first, second = halves(turned[:64]), halves(turned[64:])
        rows_ref[g * 64 : g * 64 + 64, :512] = jnp.concatenate([*first, *second], 1)
    copies[0].wait()
    for g in range(0, GROUP // 8, 4):
        found = dot(rows_ref[g * 64 : g * 64 + 256, :512], spread[...])
        for h in range(4):
            for k in range(8):
                at = (8 * (g + h) + k) * 64
                sticks_ref[at : at + 64, :] = found[h * 64 : h * 64 + 64, k * 128 : k * 128 + 128]
    copies[1].wait()

    def scatter(i, _):
        first = pl.multiple_of(i * 128, 128)
        for j in range(128):
            pltpu.store(
                square_ref.at[pl.ds(place_ref[i, j], 1), :],
                sticks_ref[pl.ds(first + j, 1), :],
                mask=mask_ref[pl.ds(first + j, 1), :] != 0.0,
            )
        return 0

    lax.fori_loop(0, STICKS // 128, scatter, 0)

    def turn(i, _):
        rows = pl.ds(pl.multiple_of(i * 128, 128), 128)
        turned_ref[rows, :] = square_ref[rows, :].T
        return 0

    lax.fori_loop(0, 32, turn, 0, unroll=4)
    pairs = [(b, p) for b in range(BANDS) for p in range(PLANES)]
    copies[2].wait()
    for k, (b, p) in enumerate(pairs):
        real = turned_ref[pl.ds(b * 16 + p, 128, stride=32), :]
        imag = turned_ref[pl.ds(b * 16 + 8 + 3 + p, 128, stride=32), :]
        rows_ref[k * 128 : k * 128 + 128, : 6 * 128] = data_rows(jnp.concatenate([real, imag], 1), 1)
        if k % 2 == 1:
            at = (k - 1) * 128
            half_ref[at : at + 256, :] = dot(rows_ref[at : at + 256, : 6 * 128], row_up[...])
    for copy in copies[3:]:
        copy.wait()
    for k, (b, p) in enumerate(pairs):
        part = half_ref[k * 128 : k * 128 + 128, :]
        part = jnp.concatenate([part[:, :FINE], part[:, FINE:]], 0)
        field = dot(col_up[...], data_rows(part, 0))
        local = pot_ref[p]
        product = field * jnp.concatenate([local, local], 0)
        part = dot(col_down[...], data_rows(product, 0))
        part = jnp.concatenate([part[:128], part[128:]], 1)
        rows_ref[k * 128 : k * 128 + 128, :] = data_rows(part, 1)
        if k % 2 == 1:
            at = (k - 1) * 128
            back_ref[at : at + 256, :] = dot(rows_ref[at : at + 256, :], row_down[...])
    for k, (b, p) in enumerate(pairs):
        for c in range(2):
            turned_ref[pl.ds(b * 16 + c * 8 + p, 128, stride=32), :] = back_ref[
                k * 128 : k * 128 + 128, c * 128 : c * 128 + 128
            ]

    def turn_back(i, _):
        rows = pl.ds(pl.multiple_of(i * 128, 128), 128)
        square_ref[rows, :] = turned_ref[rows, :].T
        return 0

    lax.fori_loop(0, 32, turn_back, 0, unroll=4)

    def gather(i, _):
        first = pl.multiple_of(i * 128, 128)
        for j in range(128):
            sticks_ref[pl.ds(first + j, 1), :] = square_ref[pl.ds(place_ref[i, j], 1), :]
        return 0

    lax.fori_loop(0, STICKS // 128, gather, 0)
    left = lane < 64
    for at in range(0, STICKS, 256):
        rows = jnp.where(mask_ref[at : at + 256, :] != 0.0, sticks_ref[at : at + 256, :], 0.0)
        found = lax.dot_general(
            choose[...],
            jnp.concatenate(halves(rows), 1),
            (((1,), (1,)), ((), ())),
            preferred_element_type=F32,
        )
        for h in range(2):
            here = found[:, h * 128 : h * 128 + 128]
            swapped = pltpu.roll(here, 64, 1)
            for i, part in enumerate(
                (jnp.where(left, here[:16], swapped[16:]), jnp.where(left, swapped[:16], here[16:]))
            ):
                to = (at // 64 + 2 * h + i) * PARTS
                send_ref[to : to + PLANES, :] = part[:PLANES]
                send_ref[to + PLANES : to + PARTS, :] = part[8 : 8 + PLANES]


def after_kernel(map_ref, corr_ref, recv_ref, down_ref, half_ref, last_ref, out_ref, next_ref):
    sticks = corr_ref.shape[1]
    kinetic = kinetic_of(map_ref, sticks)
    local = dot(down_ref[...], data_rows(recv_ref[...], 0))
    local = jnp.concatenate([local[:128].T, local[128:].T], 1)
    both = jnp.concatenate([kinetic, kinetic], 1)
    for b in range(BANDS):
        out_ref[b] = both * corr_ref[b] + local[b * sticks : (b + 1) * sticks]
        next_ref[b] = half_ref[b] + last_ref[b]


def shape(*dims):
    return jax.ShapeDtypeStruct(dims, F32)


def exchange(values):
    values = values.reshape(GROUP, 1, PARTS * 128)
    return lax.all_to_all(values, "pw", 0, 0, tiled=True).reshape(GROUP * PARTS, 128)


def in_vmem(x):
    return pltpu.with_memory_space_constraint(x, pltpu.VMEM)


def in_hbm(x):
    return pltpu.with_memory_space_constraint(x, pltpu.HBM)


def cost(us):
    return pl.CostEstimate(flops=int(us * 1e9), bytes_accessed=int(us * 3e6), transcendentals=0)


def call(kernel, name, us, inputs, out_shape, in_specs, out_specs, scratch=()):
    return pl.pallas_call(
        kernel,
        out_shape=out_shape,
        in_specs=in_specs,
        out_specs=out_specs,
        scratch_shapes=list(scratch),
        compiler_params=PARAMS,
        cost_estimate=cost(us),
        name=name,
    )(*inputs)


def middle(place, received, local, mask, t):
    grid = BANDS * PLANES * 128
    names = ("spread", "row_up", "col_up", "col_down", "row_down", "choose")
    return call(
        middle_kernel,
        "middle",
        20,
        (in_hbm(place), in_vmem(received), in_hbm(local), in_vmem(mask), *(in_hbm(t[n]) for n in names)),
        shape(GROUP * PARTS, 128),
        [ANY, VMEM, ANY, VMEM] + [ANY] * 6,
        VMEM,
        [
            pltpu.SMEM((STICKS // 128, 128), jnp.int32),
            pltpu.VMEM((PLANES, FINE, FINE), F32),
            pltpu.VMEM((STICKS, 128), F32),
            pltpu.VMEM((STICKS, 128), F32),
            pltpu.VMEM((STICKS, 128), F32),
            pltpu.VMEM((grid, 6 * FINE), BF16),
            pltpu.VMEM((grid, 2 * FINE), F32),
            pltpu.VMEM((grid, FINE), F32),
            *(pltpu.VMEM(t[n].shape, BF16) for n in names),
            pltpu.SemaphoreType.DMA((8,)),
        ],
    )


def prepare(rotation, map_rows, orbitals, correction, potential, t):
    bands, sticks, doubled = orbitals.shape
    return call(
        prepare_kernel,
        "prepare",
        7,
        tuple(
            in_hbm(x)
            for x in (rotation, map_rows, orbitals, correction, potential, t["fine_rows"], t["fine_cols"])
        ),
        (
            pltpu.HBM((PLANES, FINE, FINE), F32),
            pltpu.VMEM((STICKS, 128), F32),
            pltpu.HBM(map_rows.shape, jnp.int32),
            pltpu.HBM((2, BANDS, sticks, doubled), F32),
            pltpu.HBM((2, BANDS, sticks, doubled), F32),
        ),
        [SMEM] + [VMEM] * 3 + [ANY] + [VMEM] * 2,
        (VMEM,) * 5,
        [
            pltpu.VMEM((PLANES, LENGTH, LENGTH), F32),
            pltpu.VMEM((PLANES, 3 * LENGTH, FINE), BF16),
            pltpu.SemaphoreType.DMA((PLANES,)),
        ],
    )


def on_device(orbitals, applied_orbitals, potential, stick_map, ritz_values, ritz_rotation):
    t = {name: jnp.asarray(value) for name, value in tables().items()}
    map_rows = stick_map.reshape(-1, 128)
    sent, correction = call(
        before_kernel,
        "before",
        2,
        tuple(in_hbm(x) for x in (ritz_values, map_rows, orbitals, applied_orbitals, t["stick_up"])),
        (pltpu.HBM((GROUP * PARTS, 128), F32), pltpu.HBM(orbitals.shape, F32)),
        [SMEM] + [VMEM] * 4,
        (VMEM, VMEM),
    )
    received = exchange(sent)
    local, mask, place, kept, passed = prepare(ritz_rotation.T, map_rows, orbitals, correction, potential, t)
    came = lax.ppermute(passed, "bg", [(i, i ^ 1) for i in range(4)])
    product, came = lax.optimization_barrier((middle(place, received, local, mask, t), came))
    returned = exchange(product)
    halved = kept + came
    last = lax.ppermute(halved[1], "bg", [(i, 3 - i) for i in range(4)])
    applied_correction, next_orbitals = call(
        after_kernel,
        "after",
        2,
        (in_hbm(map_rows), in_hbm(correction), in_vmem(returned), in_hbm(t["stick_down"]), halved[0], last),
        (shape(*orbitals.shape), shape(*orbitals.shape)),
        [VMEM] * 6,
        (VMEM, VMEM),
    )
    return (next_orbitals, applied_correction)


def solution(mesh):
    return jax.shard_map(
        on_device,
        mesh=mesh,
        in_specs=(P("bg", "pw", None), P("bg", "pw", None), P("pw", None, None), P(), P("bg"), P()),
        out_specs=(P("bg", "pw", None), P("bg", "pw", None)),
        check_vma=False,
    )
```

time: 93.1 us -> 69.6 us (0.75)
  blocking collectives: 17.7 us -> 0 us
  starting transfers between devices: 10.4 us -> 26.1 us
  between operations: 14 us -> 0.7 us
  Pallas kernels: 45.5 us -> 35.4 us
  waiting for transfers between devices: 2.44 us -> 7 us
  local copies, waits for them, and re-layouts: 2.08 us -> 0.02 us
    all_to_all x1 -> x0, blocking collectives: 17.7 us -> none  [exchange(): lax.all_to_all(values, 'pw', 0, 0, tiled=True).reshape(GROUP * PARTS, 128)]
    pallas_call x4, Pallas kernels: 45.5 us -> 35.4 us  [call(): pl.pallas_call(kernel, out_shape=out_shape, in_specs=in_specs, out_specs=...]
    all_to_all x1 -> x2, starting transfers between devices: 10.3 us -> 19.5 us  [exchange(): lax.all_to_all(values, 'pw', 0, 0, tiled=True).reshape(GROUP * PARTS, 128)]
    ppermute x0 -> x2, waiting for transfers between devices: none -> 6.84 us  [the longest x1 6.84 us: on_device(): last = lax.ppermute(halved[1], 'bg', [(i, 3 - i) for i in range(4)])]
    ppermute x0 -> x2, starting transfers between devices: none -> 6.65 us  [the longest x1 3.39 us: on_device(): last = lax.ppermute(halved[1], 'bg', [(i, 3 - i) for i in range(4)])]
    unnamed x5 -> x2, local copies, waits for them, and re-layouts: 2.08 us -> 0.01 us
    all_to_all x1 -> x2, waiting for transfers between devices: 1.77 us -> 0.16 us  [exchange(): lax.all_to_all(values, 'pw', 0, 0, tiled=True).reshape(GROUP * PARTS, 128)]
  transfers between devices with their start and end apart: 2 -> 4, of which waited for: 1 -> 2; matrix products, arithmetic and copies ran while one was open for 1% -> 0% of each run, Pallas kernels for 46% -> 44%
where the time goes in v1:
time: 69.6 us; the launch traced here: 69.3 us
  Pallas kernels  35.4 us (51%)
  starting transfers between devices  26.1 us (38%)
  waiting for transfers between devices  7 us (10%)
  between operations  0.7 us (1%)
    pallas_call x4, Pallas kernels, call(): pl.pallas_call(kernel, out_shape=out_shape, in_specs=in_specs, out_specs=...  35.4 us
    all_to_all x2, starting transfers between devices, exchange(): lax.all_to_all(values, 'pw', 0, 0, tiled=True).reshape(GROUP * PARTS, 128)  19.5 us
    ppermute x1, waiting for transfers between devices, on_device(): last = lax.ppermute(halved[1], 'bg', [(i, 3 - i) for i in range(4)])  6.84 us
    ppermute x1, starting transfers between devices, on_device(): last = lax.ppermute(halved[1], 'bg', [(i, 3 - i) for i in range(4)])  3.39 us
    ppermute x1, starting transfers between devices, on_device(): came = lax.ppermute(passed, 'bg', [(i, i ^ 1) for i in range(4)])  3.26 us
  transfers between devices with their start and end apart: 4, of which 2 were waited for; matrix products, arithmetic and copies ran while one was open for 0% of the time, Pallas kernels for 44%

profile of v1, /device:TPU:1, one launch (start us, length us, event | category | flops | bytes accessed | tf_op | source)
XLA Modules:
  0.0 69.3 jit_solution(5919375436402937746)
XLA Ops:
  0.6 2.7 %before.1 = (f32[640,128]{1,0:T(8,128)}, f32[2,64,256]{2,1,0:T(8,128)}) custom-call(f32[2]{0:T(128)} %values_ref.1, s32[32,128]{1,0:T(8,128)} %bitcast.13, f32[2,64,256]{2,1,0:T(8,128)} %orb_ref.3, f32[2,64,256]{2,1,0:T(8,128)} %app_ref.1, bf16[640,768]{1,0:T(8,128)(2,1)} %constant.24.clone.up_ref), custom_call_target="tpu_custom_call" | custom-call | flops 2000000000 | bytes 6000000 | tf_op jit(solution)/shard_map/before/pallas_call | solution.py:337
  3.4 10.3 %all-to-all-start = ((f32[64,1,1280]{2,1,0:T(1,128)}), f32[64,1,1280]{2,1,0:T(1,128)S(1)}, u32[]{:S(2)}, u32[]{:S(2)}) async-start(f32[64,1,1280]{2,1,0:T(1,128)} %bitcast.12), calls=%async_computation | async-start | bytes 655360 | tf_op jit(solution)/shard_map/all_to_all | solution.py:321
  13.7 8.0 %prepare.1 = (f32[5,256,256]{2,1,0:T(8,128)}, f32[4096,128]{1,0:T(8,128)S(1)}, s32[32,128]{1,0:T(8,128)}, f32[2,2,64,256]{3,2,1,0:T(8,128)}, f32[2,2,64,256]{3,2,1,0:T(8,128)}) custom-call(f32[8,16]{1,0:T(8,128)} %bitcast.16, s32[32,128]{1,0:T(8,128)} %bitcast.14, f32[2,64,256]{2,1,0:T(8,128)} %orb_ref.3, f32[2,64,256]{2,1,0:T(8,128)} %get-tuple-element.13.corr_ref, ...), custom_call_target="tpu_custom_call" | custom-call | flops 7000000000 | bytes 21000000 | tf_op jit(solution)/shard_map/prepare/pallas_call | solution.py:337
  21.7 3.3 %collective-permute-start = (f32[2,2,64,256]{3,2,1,0:T(8,128)}, f32[2,2,64,256]{3,2,1,0:T(8,128)S(1)}, u32[]{:S(2)}, u32[]{:S(2)}) collective-permute-start(f32[2,2,64,256]{3,2,1,0:T(8,128)} %get-tuple-element.18), channel_id=1, source_target_pairs={{0,64},{64,0},{128,192},{192,128},{1,65},{65,1},{129,193},{193,129... | collective-permute-start | bytes 786440 | tf_op jit(solution)/shard_map/ppermute | solution.py:416
  25.0 0.0 all-to-all-done
  25.0 0.0 copy-start
  25.0 22.2 %middle.1 = f32[640,128]{1,0:T(8,128)} custom-call(s32[32,128]{1,0:T(8,128)} %get-tuple-element.14.place_hbm, f32[640,128]{1,0:T(8,128)S(1)} %bitcast.11, f32[5,256,256]{2,1,0:T(8,128)} %get-tuple-element.16.pot_hbm, f32[4096,128]{1,0:T(8,128)S(1)} %get-tuple-element.17.mask_ref, bf16[512,1024]{1,0:T(8,128)(2,1)} %constant.27.clone.spread_hbm, ...), custom_call_target="tpu_custom_call" | custom-call | flops 20000000000 | bytes 60000000 | tf_op jit(solution)/shard_map/middle/pallas_call | solution.py:337
  47.2 0.0 collective-permute-done
  47.2 9.1 %all-to-all-start.1 = ((f32[64,1,1280]{2,1,0:T(1,128)}), f32[64,1,1280]{2,1,0:T(1,128)S(1)}, u32[]{:S(2)}, u32[]{:S(2)}) async-start(f32[64,1,1280]{2,1,0:T(1,128)} %bitcast.4), calls=%async_computation.1 | async-start | bytes 655360 | tf_op jit(solution)/shard_map/all_to_all | solution.py:321
  56.3 0.0 copy-done
  56.4 3.4 %collective-permute-start.1 = (f32[2,64,256]{2,1,0:T(8,128)S(1)}, f32[2,64,256]{2,1,0:T(8,128)S(1)}, u32[]{:S(2)}, u32[]{:S(2)}) collective-permute-start(f32[2,64,256]{2,1,0:T(8,128)S(1)} %get-tuple-element.24), channel_id=1, source_target_pairs={{0,192},{64,128},{128,64},{192,0},{1,193},{65,129},{129,65},{193,1... | collective-permute-start | bytes 393224 | tf_op jit(solution)/shard_map/ppermute | solution.py:420
  59.8 6.8 %collective-permute-done.1.last_ref = f32[2,64,256]{2,1,0:T(8,128)S(1)} collective-permute-done((f32[2,64,256]{2,1,0:T(8,128)S(1)}, f32[2,64,256]{2,1,0:T(8,128)S(1)}, u32[]{:S(2)}, u32[]{:S(2)}) %collective-permute-start.1) | collective-permute-done | bytes 131104 | tf_op jit(solution)/shard_map/ppermute | solution.py:420
  66.7 0.2 all-to-all-done.1
  66.8 2.5 %after.1 = (f32[2,64,256]{2,1,0:T(8,128)}, f32[2,64,256]{2,1,0:T(8,128)}) custom-call(s32[32,128]{1,0:T(8,128)} %bitcast.15, f32[2,64,256]{2,1,0:T(8,128)} %get-tuple-element.13.corr_ref, f32[640,128]{1,0:T(8,128)S(1)} %bitcast.10, bf16[256,1920]{1,0:T(8,128)(2,1)} %constant.25.clone.down_ref, f32[2,64,256]{2,1,0:T(8,128)S(1)} %get-tuple-element.25.half_ref, ...), custom_call_target="tpu_custom_call" | custom-call | flops 2000000000 | bytes 6000000 | tf_op jit(solution)/shard_map/after/pallas_call | solution.py:337
  (2 shorter events, 0.1 us)
Async XLA Ops:
  3.4 21.6 %all-to-all-start = ((f32[64,1,1280]{2,1,0:T(1,128)}), f32[64,1,1280]{2,1,0:T(1,128)S(1)}, u32[]{:S(2)}, u32[]{:S(2)}) async-start(f32[64,1,1280]{2,1,0:T(1,128)} %bitcast.12), calls=%async_computation | async-start | bytes 655360 | tf_op jit(solution)/shard_map/all_to_all | solution.py:321
  21.7 25.5 %collective-permute-start = (f32[2,2,64,256]{3,2,1,0:T(8,128)}, f32[2,2,64,256]{3,2,1,0:T(8,128)S(1)}, u32[]{:S(2)}, u32[]{:S(2)}) collective-permute-start(f32[2,2,64,256]{3,2,1,0:T(8,128)} %get-tuple-element.18), channel_id=1, source_target_pairs={{0,64},{64,0},{128,192},{192,128},{1,65},{65,1},{129,193},{193,129... | collective-permute-start | bytes 786440 | tf_op jit(solution)/shard_map/ppermute | solution.py:416
  25.0 31.4 %copy-start = (f32[2,2,64,256]{3,2,1,0:T(8,128)S(1)}, f32[2,2,64,256]{3,2,1,0:T(8,128)}, u32[]{:S(2)}) copy-start(f32[2,2,64,256]{3,2,1,0:T(8,128)} %get-tuple-element.20) | copy-start | bytes 786436
  47.2 19.6 %all-to-all-start.1 = ((f32[64,1,1280]{2,1,0:T(1,128)}), f32[64,1,1280]{2,1,0:T(1,128)S(1)}, u32[]{:S(2)}, u32[]{:S(2)}) async-start(f32[64,1,1280]{2,1,0:T(1,128)} %bitcast.4), calls=%async_computation.1 | async-start | bytes 655360 | tf_op jit(solution)/shard_map/all_to_all | solution.py:321
  56.4 10.2 %collective-permute-start.1 = (f32[2,64,256]{2,1,0:T(8,128)S(1)}, f32[2,64,256]{2,1,0:T(8,128)S(1)}, u32[]{:S(2)}, u32[]{:S(2)}) collective-permute-start(f32[2,64,256]{2,1,0:T(8,128)S(1)} %get-tuple-element.24), channel_id=1, source_target_pairs={{0,192},{64,128},{128,64},{192,0},{1,193},{65,129},{129,65},{193,1... | collective-permute-start | bytes 393224 | tf_op jit(solution)/shard_map/ppermute | solution.py:420

commit v2 on v1

--- a/solution.py
+++ b/solution.py
@@ -15,7 +15,7 @@
 VMEM = pl.BlockSpec(memory_space=pltpu.VMEM)
 SMEM = pl.BlockSpec(memory_space=pltpu.SMEM)
 ANY = pl.BlockSpec(memory_space=pl.ANY)
-PARAMS = pltpu.CompilerParams(vmem_limit_bytes=40 * 1024 * 1024)
+PARAMS = pltpu.CompilerParams(vmem_limit_bytes=32 * 1024 * 1024)
 
 LENGTH = 320
 WIDTH = 128
@@ -33,17 +33,65 @@
     return high, low
 
 
-def complex_table(length):
-    frequencies = np.arange(WIDTH) - WIDTH // 2
-    angles = 2.0 * math.pi * (np.outer(frequencies, np.arange(length)) % length) / length
+HALF = WIDTH // 2
+
+
+def frequency_slots():
+    return np.concatenate([np.arange(HALF), [-HALF], -np.arange(1, HALF)])
+
+
+def point_slots():
+    return np.concatenate([np.arange(WIDTH), [WIDTH], -np.arange(1, WIDTH)])
+
+
+def complex_table(frequencies, points, length):
+    angles = 2.0 * math.pi * (np.outer(frequencies, points) % length) / length
     cosine, sine = np.cos(angles) / math.sqrt(length), np.sin(angles) / math.sqrt(length)
     return np.concatenate(
         [np.concatenate([cosine, sine], 1), np.concatenate([-sine, cosine], 1)], 0
     )
 
 
+def wave(function, frequencies, points):
+    angles = 2.0 * math.pi * (np.outer(frequencies, points) % FINE) / FINE
+    return function(angles) / math.sqrt(FINE)
+
+
+def folded_tables():
+    zeros = np.zeros
+    pairs, near = np.arange(HALF), np.arange(WIDTH)
+    three = np.concatenate
+
+    def joined(main, single):
+        high, low = split_host(main)
+        return three([high, high, low, single.astype(ml_dtypes.bfloat16)], 1)
+
+    points = point_slots()
+    sines = -wave(np.sin, pairs, points)
+    sines[0] = wave(np.sin, [HALF], points)
+    single = zeros((FINE, WIDTH))
+    single[:, 0] = single[:, HALF] = wave(np.cos, [HALF], points)[0]
+    row_up = joined(three([wave(np.cos, pairs, points), sines], 0).T, single).T
+    single = zeros((WIDTH + 16, 16))
+    single[: WIDTH + 1, 0] = single[: WIDTH + 1, 8] = wave(np.cos, [HALF], np.arange(WIDTH + 1))[0]
+    even = zeros((WIDTH + 16, HALF))
+    even[: WIDTH + 1] = wave(np.cos, pairs, np.arange(WIDTH + 1)).T
+    even_up = joined(even, single)
+    single = zeros((WIDTH, 16))
+    single[:, 0] = single[:, 8] = -wave(np.sin, [HALF], near)[0]
+    odd_up = joined(wave(np.sin, pairs, near).T, single)
+    single = zeros((HALF + 16, 16))
+    single[: HALF + 1, 0] = single[: HALF + 1, 8] = wave(np.cos, np.arange(HALF + 1), [WIDTH])[:, 0]
+    even = zeros((HALF + 16, WIDTH))
+    even[: HALF + 1] = wave(np.cos, np.arange(HALF + 1), near)
+    even_down = joined(even, single)
+    odd_high, odd_low = split_host(wave(np.sin, [HALF, *range(1, HALF)], near))
+    odd_down = three([odd_high, odd_high, odd_low], 1)
+    return dict(row_up=row_up, even_up=even_up, odd_up=odd_up, even_down=even_down, odd_down=odd_down)
+
+
 def resampling_table():
-    places = np.arange(FINE)[:, None] * LENGTH - np.arange(LENGTH)[None, :] * FINE
+    places = point_slots()[:, None] * LENGTH - np.arange(LENGTH)[None, :] * FINE
     total = np.zeros((FINE, LENGTH))
     for d in range(-(WIDTH - 1), WIDTH):
         total += np.cos(2.0 * math.pi * ((places * d) % (FINE * LENGTH)) / (FINE * LENGTH))
@@ -68,18 +116,15 @@
 
 
 def tables():
-    square = complex_table(FINE)
-    high, low = split_host(square)
-    stick = complex_table(LENGTH).reshape(2 * WIDTH, 2, GROUP, PLANES)
+    high, low = split_host(complex_table(frequency_slots(), point_slots(), FINE))
+    stick = complex_table(np.arange(WIDTH) - HALF, np.arange(LENGTH), LENGTH).reshape(2 * WIDTH, 2, GROUP, PLANES)
     stick = stick.transpose(0, 2, 1, 3).reshape(2 * WIDTH, GROUP * PARTS)
     s_high, s_low = split_host(stick)
     r_high, r_low = split_host(resampling_table())
     three = np.concatenate
     return dict(
-        row_up=three([high, high, low], 0),
+        **folded_tables(),
         row_down=three([high.T, high.T, low.T], 0),
-        col_up=three([high.T, low.T, high.T], 1),
-        col_down=three([high, low, high], 1),
         stick_up=three([s_high.T, s_low.T, s_high.T], 1),
         stick_down=three([s_high, s_low, s_high], 1),
         fine_cols=three([r_high, r_low, r_high], 1),
@@ -102,6 +147,30 @@
 
 def dot(a, b):
     return jnp.dot(a, b, preferred_element_type=F32)
+
+
+def slot_of(index):
+    return jnp.where(index >= HALF, index - HALF, HALF + ((HALF - index) & (HALF - 1)))
+
+
+def bare_first(x):
+    first = lax.broadcasted_iota(jnp.int32, (8, 1), 0) == 0
+    return jnp.concatenate([jnp.where(first, 0.0, x[:8]), x[8:]], 0)
+
+
+def other_first(x, other):
+    first = lax.broadcasted_iota(jnp.int32, (8, 1), 0) == 0
+    return jnp.concatenate([jnp.where(first, other[:8], x[:8]), x[8:]], 0)
+
+
+def folded_data(x, single=None):
+    high, low = halves(x)
+    parts = [high, low, high]
+    if single is not None:
+        top = single[:8]
+        top_high = top.astype(BF16).astype(F32)
+        parts.append(jnp.concatenate([top_high, top - top_high], 0).astype(BF16))
+    return jnp.concatenate(parts, 0)
 
 
 def planar_of(map_ref, sticks):
@@ -137,13 +206,14 @@
 
 
 def prepare_kernel(
-    rotation_ref, map_ref, orb_ref, corr_ref, pot_hbm, rows_ref, cols_ref, out_ref, mask_ref, place_ref, keep_ref, pass_ref,
+    rotation_ref, map_ref, orb_ref, corr_ref, pot_hbm, rows_ref, cols_ref, out_ref, bits_ref, place_ref, keep_ref, pass_ref,
     pot_ref, work_ref, sems,
 ):
-    copies = []
-    for p in range(PLANES):
-        copies.append(pltpu.make_async_copy(pot_hbm.at[p], pot_ref.at[p], sems.at[p]))
-        copies[-1].start()
+    copies = [
+        pltpu.make_async_copy(pot_hbm.at[p], pot_ref.at[pl.ds(p * LENGTH, LENGTH), :], sems.at[p]) for p in range(PLANES)
+    ]
+    for copy in copies:
+        copy.start()
     me = lax.axis_index("bg")
     all_bands = rotation_ref.shape[0]
     for target, group in ((keep_ref, me), (pass_ref, me ^ 1)):
@@ -156,33 +226,44 @@
                     term = term + rotation_ref[j, all_bands + me * BANDS + b] * corr_ref[b]
                     total = term if total is None else total + term
                 target[k, i] = total
-    place_ref[...] = ((map_ref[...] >> 9) << 7) | (map_ref[...] & 127)
-    lane_block = lax.broadcasted_iota(jnp.int32, (128, 128), 1) >> 5
-
-    def mark(i, _):
-        blocks = jnp.broadcast_to((map_ref[pl.ds(i, 1), :] >> 7) & 3, (128, 128)).T
-        mask_ref[pl.ds(pl.multiple_of(i * 128, 128), 128), :] = jnp.where(blocks == lane_block, 1.0, 0.0)
-        return 0
-
-    lax.fori_loop(0, STICKS // 128, mark, 0, unroll=4)
+    columns = slot_of(map_ref[...] >> 7)
+    place_ref[...] = ((columns >> 2) << 7) | slot_of(map_ref[...] & 127)
+    columns = columns & 3
+    row_block = lax.broadcasted_iota(jnp.int32, (128, 128), 0) >> 5
+    stick = lax.broadcasted_iota(jnp.int32, (16, 128), 1)
+    eight = lax.broadcasted_iota(jnp.int32, (16, 128), 0)
+    weights = jnp.where((stick >> 3) == eight, (1 << (stick & 7)).astype(F32), 0.0).astype(BF16)
     rows_high, rows_low = rows_ref[0], rows_ref[1]
-    for p in range(PLANES):
-        copies[p].wait()
-        for at in range(0, LENGTH, LENGTH // 2):
-            high, low = halves(pot_ref[p, at : at + LENGTH // 2, :])
-            part = dot(high, rows_high) + (dot(low, rows_high) + dot(high, rows_low))
-            high, low = halves(part)
-            work_ref[p, at : at + LENGTH // 2] = high
-            work_ref[p, LENGTH + at : LENGTH + at + LENGTH // 2] = high
-            work_ref[p, 2 * LENGTH + at : 2 * LENGTH + at + LENGTH // 2] = low
-        out_ref[p] = dot(cols_ref[...], work_ref[p])
+    marked = arrived = done = 0
+    for at in range(0, PLANES * LENGTH, 256):
+        end = min(at + 256, PLANES * LENGTH)
+        while arrived * LENGTH < end:
+            copies[arrived].wait()
+            arrived += 1
+        high, low = halves(pot_ref[at:end, :])
+        part = dot(high, rows_high) + (dot(low, rows_high) + dot(high, rows_low))
+        high, low = halves(part)
+        for p in range(at // LENGTH, (end - 1) // LENGTH + 1):
+            first, stop = max(at, p * LENGTH), min(end, (p + 1) * LENGTH)
+            for k, values in enumerate((high, high, low)):
+                to = k * LENGTH + first - p * LENGTH
+                work_ref[p, to : to + stop - first] = values[first - at : stop - at]
+        while (done + 1) * LENGTH <= end:
+            out_ref[done] = dot(cols_ref[...], work_ref[done])
+            done += 1
+        while marked < STICKS // 128 and marked < (at // 256 + 1) * 5:
+            match = jnp.where(columns[marked : marked + 1, :] == row_block, 1.0, 0.0).astype(BF16)
+            bits = lax.dot_general(weights, match, (((1,), (1,)), ((), ())), preferred_element_type=F32)
+            bits_ref[marked * 16 : marked * 16 + 16, :] = bits.astype(jnp.int32)
+            marked += 1
 
 
 def middle_kernel(
-    place_hbm, recv_ref, pot_hbm, mask_ref, spread_hbm, row_up_hbm, col_up_hbm, col_down_hbm, row_down_hbm, choose_hbm,
+    place_hbm, recv_ref, pot_ref, bits_ref, spread_hbm, row_up_hbm, even_up_hbm, odd_up_hbm, even_down_hbm,
+    odd_down_hbm, row_down_hbm, choose_hbm,
     send_ref,
-    place_ref, pot_ref, sticks_ref, square_ref, turned_ref, rows_ref, half_ref, back_ref,
-    spread, row_up, col_up, col_down, row_down, choose, sems,
+    place_ref, sticks_ref, square_ref, turned_ref, rows_ref, half_ref, back_ref,
+    spread, row_up, even_up, odd_up, even_down, odd_down, row_down, choose, sems,
 ):
     copies = [
         pltpu.make_async_copy(source, target, sems.at[i])
@@ -191,9 +272,10 @@
                 (spread_hbm, spread),
                 (place_hbm, place_ref),
                 (row_up_hbm, row_up),
-                (pot_hbm, pot_ref),
-                (col_up_hbm, col_up),
-                (col_down_hbm, col_down),
+                (even_up_hbm, even_up),
+                (odd_up_hbm, odd_up),
+                (even_down_hbm, even_down),
+                (odd_down_hbm, odd_down),
                 (row_down_hbm, row_down),
                 (choose_hbm, choose),
             )
@@ -226,7 +308,7 @@
             pltpu.store(
                 square_ref.at[pl.ds(place_ref[i, j], 1), :],
                 sticks_ref[pl.ds(first + j, 1), :],
-                mask=mask_ref[pl.ds(first + j, 1), :] != 0.0,
+                mask=(bits_ref[pl.ds(i * 16 + j // 8, 1), :] & (1 << (j % 8))) != 0,
             )
         return 0
 
@@ -240,24 +322,57 @@
     lax.fori_loop(0, 32, turn, 0, unroll=4)
     pairs = [(b, p) for b in range(BANDS) for p in range(PLANES)]
     copies[2].wait()
+    left = lane < HALF
+    alone = (lane & (HALF - 1)) == 0
     for k, (b, p) in enumerate(pairs):
-        real = turned_ref[pl.ds(b * 16 + p, 128, stride=32), :]
-        imag = turned_ref[pl.ds(b * 16 + 8 + 3 + p, 128, stride=32), :]
-        rows_ref[k * 128 : k * 128 + 128, : 6 * 128] = data_rows(jnp.concatenate([real, imag], 1), 1)
+        sums = []
+        ends = []
+        for at in (b * 16 + p, b * 16 + 8 + 3 + p):
+            x = turned_ref[pl.ds(at, 128, stride=32), :]
+            mirror = pltpu.roll(x, HALF, 1)
+            sums.append(jnp.where(alone, x, jnp.where(left, x, -x) + mirror))
+            end = jnp.where(left, mirror, x)
+            end_high = end.astype(BF16).astype(F32)
+            ends.append(jnp.where(left, end - end_high, end_high).astype(BF16))
+        real, imag = sums
+        for i, x in enumerate((jnp.where(left, real, imag), jnp.where(left, imag, -real))):
+            high, low = halves(x)
+            rows_ref[k * 128 : k * 128 + 128, i * 512 : i * 512 + 512] = jnp.concatenate([high, low, high, ends[i]], 1)
         if k % 2 == 1:
             at = (k - 1) * 128
-            half_ref[at : at + 256, :] = dot(rows_ref[at : at + 256, : 6 * 128], row_up[...])
+            for i in range(2):
+                half_ref[at : at + 256, i * FINE : i * FINE + FINE] = dot(
+                    rows_ref[at : at + 256, i * 512 : i * 512 + 512], row_up[...]
+                )
     for copy in copies[3:]:
         copy.wait()
     for k, (b, p) in enumerate(pairs):
-        part = half_ref[k * 128 : k * 128 + 128, :]
-        part = jnp.concatenate([part[:, :FINE], part[:, FINE:]], 0)
-        field = dot(col_up[...], data_rows(part, 0))
+        upper = half_ref[k * 128 : k * 128 + HALF, :]
+        lower = half_ref[k * 128 + HALF : k * 128 + 128, :]
+        even = dot(even_up[...], folded_data(upper + bare_first(lower), lower))
+        odd = dot(odd_up[...], folded_data(upper - lower, lower))
+        odd_real, odd_imag = odd[:, :FINE], odd[:, FINE:]
         local = pot_ref[p]
-        product = field * jnp.concatenate([local, local], 0)
-        part = dot(col_down[...], data_rows(product, 0))
-        part = jnp.concatenate([part[:128], part[128:]], 1)
-        rows_ref[k * 128 : k * 128 + 128, :] = data_rows(part, 1)
+        last = even[WIDTH : WIDTH + 8]
+        even = even[:WIDTH]
+        ahead = jnp.concatenate([even[:, :FINE] - odd_imag, even[:, FINE:] + odd_real], 1)
+        behind = jnp.concatenate([even[:, :FINE] + odd_imag, even[:, FINE:] - odd_real], 1)
+        behind = other_first(behind, last)
+        ahead = ahead * jnp.concatenate([local[:WIDTH], local[:WIDTH]], 1)
+        behind = behind * jnp.concatenate([local[WIDTH:], local[WIDTH:]], 1)
+        even = dot(even_down[...], folded_data(ahead + bare_first(behind), behind))
+        odd = dot(odd_down[...], folded_data(ahead - behind))
+        odd_plus = bare_first(odd)
+        last = even[HALF : HALF + 8]
+        even = even[:HALF]
+        even_minus = other_first(even, last)
+        real = jnp.concatenate(
+            [even[:, :FINE] + odd_plus[:, FINE:], even_minus[:, :FINE] - odd[:, FINE:]], 0
+        )
+        imag = jnp.concatenate(
+            [even[:, FINE:] - odd_plus[:, :FINE], even_minus[:, FINE:] + odd[:, :FINE]], 0
+        )
+        rows_ref[k * 128 : k * 128 + 128, :] = data_rows(jnp.concatenate([real, imag], 1), 1)
         if k % 2 == 1:
             at = (k - 1) * 128
             back_ref[at : at + 256, :] = dot(rows_ref[at : at + 256, :], row_down[...])
@@ -281,9 +396,10 @@
         return 0
 
     lax.fori_loop(0, STICKS // 128, gather, 0)
-    left = lane < 64
+    own_bit = 1 << (lax.broadcasted_iota(jnp.int32, (256, 128), 0) & 7)
     for at in range(0, STICKS, 256):
-        rows = jnp.where(mask_ref[at : at + 256, :] != 0.0, sticks_ref[at : at + 256, :], 0.0)
+        bits = jnp.broadcast_to(bits_ref[at // 8 : at // 8 + 32, :][:, None, :], (32, 8, 128)).reshape(256, 128)
+        rows = jnp.where((bits & own_bit) != 0, sticks_ref[at : at + 256, :], 0.0)
         found = lax.dot_general(
             choose[...],
             jnp.concatenate(halves(rows), 1),
@@ -301,7 +417,7 @@
                 send_ref[to + PLANES : to + PARTS, :] = part[8 : 8 + PLANES]
 
 
-def after_kernel(map_ref, corr_ref, recv_ref, down_ref, half_ref, last_ref, out_ref, next_ref):
+def after_kernel(map_ref, corr_ref, recv_ref, down_ref, out_ref):
     sticks = corr_ref.shape[1]
     kinetic = kinetic_of(map_ref, sticks)
     local = dot(down_ref[...], data_rows(recv_ref[...], 0))
@@ -309,7 +425,6 @@
     both = jnp.concatenate([kinetic, kinetic], 1)
     for b in range(BANDS):
         out_ref[b] = both * corr_ref[b] + local[b * sticks : (b + 1) * sticks]
-        next_ref[b] = half_ref[b] + last_ref[b]
 
 
 def shape(*dims):
@@ -348,18 +463,17 @@
 
 def middle(place, received, local, mask, t):
     grid = BANDS * PLANES * 128
-    names = ("spread", "row_up", "col_up", "col_down", "row_down", "choose")
+    names = ("spread", "row_up", "even_up", "odd_up", "even_down", "odd_down", "row_down", "choose")
     return call(
         middle_kernel,
         "middle",
         20,
-        (in_hbm(place), in_vmem(received), in_hbm(local), in_vmem(mask), *(in_hbm(t[n]) for n in names)),
-        shape(GROUP * PARTS, 128),
-        [ANY, VMEM, ANY, VMEM] + [ANY] * 6,
+        (in_hbm(place), in_vmem(received), in_vmem(local), in_vmem(mask), *(in_hbm(t[n]) for n in names)),
+        pltpu.VMEM((GROUP * PARTS, 128), F32),
+        [ANY, VMEM, VMEM, VMEM] + [ANY] * 8,
         VMEM,
         [
             pltpu.SMEM((STICKS // 128, 128), jnp.int32),
-            pltpu.VMEM((PLANES, FINE, FINE), F32),
             pltpu.VMEM((STICKS, 128), F32),
             pltpu.VMEM((STICKS, 128), F32),
             pltpu.VMEM((STICKS, 128), F32),
@@ -367,7 +481,7 @@
             pltpu.VMEM((grid, 2 * FINE), F32),
             pltpu.VMEM((grid, FINE), F32),
             *(pltpu.VMEM(t[n].shape, BF16) for n in names),
-            pltpu.SemaphoreType.DMA((8,)),
+            pltpu.SemaphoreType.DMA((9,)),
         ],
     )
 
@@ -383,16 +497,16 @@
             for x in (rotation, map_rows, orbitals, correction, potential, t["fine_rows"], t["fine_cols"])
         ),
         (
-            pltpu.HBM((PLANES, FINE, FINE), F32),
-            pltpu.VMEM((STICKS, 128), F32),
+            pltpu.VMEM((PLANES, FINE, FINE), F32),
+            pltpu.VMEM((STICKS // 8, 128), jnp.int32),
             pltpu.HBM(map_rows.shape, jnp.int32),
-            pltpu.HBM((2, BANDS, sticks, doubled), F32),
-            pltpu.HBM((2, BANDS, sticks, doubled), F32),
+            pltpu.VMEM((2, BANDS, sticks, doubled), F32),
+            pltpu.VMEM((2, BANDS, sticks, doubled), F32),
         ),
-        [SMEM] + [VMEM] * 3 + [ANY] + [VMEM] * 2,
+        [SMEM, VMEM, VMEM, VMEM, ANY, VMEM, VMEM],
         (VMEM,) * 5,
         [
-            pltpu.VMEM((PLANES, LENGTH, LENGTH), F32),
+            pltpu.VMEM((PLANES * LENGTH, LENGTH), F32),
             pltpu.VMEM((PLANES, 3 * LENGTH, FINE), BF16),
             pltpu.SemaphoreType.DMA((PLANES,)),
         ],
@@ -407,7 +521,7 @@
         "before",
         2,
         tuple(in_hbm(x) for x in (ritz_values, map_rows, orbitals, applied_orbitals, t["stick_up"])),
-        (pltpu.HBM((GROUP * PARTS, 128), F32), pltpu.HBM(orbitals.shape, F32)),
+        (pltpu.VMEM((GROUP * PARTS, 128), F32), pltpu.HBM(orbitals.shape, F32)),
         [SMEM] + [VMEM] * 4,
         (VMEM, VMEM),
     )
@@ -418,15 +532,17 @@
     returned = exchange(product)
     halved = kept + came
     last = lax.ppermute(halved[1], "bg", [(i, 3 - i) for i in range(4)])
-    applied_correction, next_orbitals = call(
+    applied_correction = call(
         after_kernel,
         "after",
         2,
-        (in_hbm(map_rows), in_hbm(correction), in_vmem(returned), in_hbm(t["stick_down"]), halved[0], last),
-        (shape(*orbitals.shape), shape(*orbitals.shape)),
-        [VMEM] * 6,
-        (VMEM, VMEM),
-    )
+        (in_vmem(map_rows), in_vmem(correction), in_vmem(returned), in_vmem(t["stick_down"])),
+        shape(*orbitals.shape),
+        [VMEM] * 4,
+        VMEM,
+    )
+    applied_correction, last = lax.optimization_barrier((applied_correction, last))
+    next_orbitals = halved[0] + last
     return (next_orbitals, applied_correction)
 
 

time: 69.6 us -> 66.3 us (0.953)
  Pallas kernels: 35.4 us -> 31.4 us
  other arithmetic: 0.04 us -> 1.66 us
  waiting for transfers between devices: 7 us -> 6.08 us
    ppermute x1, waiting for transfers between devices: 6.84 us -> 0.01 us  [on_device(): last = lax.ppermute(halved[1], 'bg', [(i, 3 - i) for i in range(4)])]
    all_to_all x2, waiting for transfers between devices: 0.16 us -> 6.08 us  [exchange(): lax.all_to_all(values, 'pw', 0, 0, tiled=True).reshape(GROUP * PARTS, 128)]
    pallas_call x4, Pallas kernels: 35.4 us -> 31.4 us  [call(): pl.pallas_call(kernel, out_shape=out_shape, in_specs=in_specs, out_specs=...]
    add x1, other arithmetic: 0.04 us -> 0.99 us  [on_device(): halved = kept + came]
  transfers between devices with their start and end apart: 4 -> 4, of which waited for: 2 -> 1; matrix products, arithmetic and copies ran while one was open for 0% -> 2% of each run, Pallas kernels for 44% -> 43%
where the time goes in v2:
time: 66.3 us; the launch traced here: 66 us
  Pallas kernels  31.4 us (47%)
  starting transfers between devices  26.1 us (39%)
  waiting for transfers between devices  6.08 us (9%)
  other arithmetic  1.66 us (3%)
  between operations  0.7 us (1%)
    pallas_call x4, Pallas kernels, call(): pl.pallas_call(kernel, out_shape=out_shape, in_specs=in_specs, out_specs=...  31.4 us
    all_to_all x2, starting transfers between devices, exchange(): lax.all_to_all(values, 'pw', 0, 0, tiled=True).reshape(GROUP * PARTS, 128)  19.5 us
    all_to_all x2, waiting for transfers between devices, exchange(): lax.all_to_all(values, 'pw', 0, 0, tiled=True).reshape(GROUP * PARTS, 128)  6.08 us
    ppermute x1, starting transfers between devices, on_device(): last = lax.ppermute(halved[1], 'bg', [(i, 3 - i) for i in range(4)])  3.39 us
    ppermute x1, starting transfers between devices, on_device(): came = lax.ppermute(passed, 'bg', [(i, i ^ 1) for i in range(4)])  3.26 us
  transfers between devices with their start and end apart: 4, of which 1 were waited for; matrix products, arithmetic and copies ran while one was open for 2% of the time, Pallas kernels for 43%

profile of v2, /device:TPU:1, one launch (start us, length us, event | category | flops | bytes accessed | tf_op | source)
XLA Modules:
  0.0 66.0 jit_solution(5311053405990322015)
XLA Ops:
  0.6 2.7 %before.1 = (f32[640,128]{1,0:T(8,128)}, f32[2,64,256]{2,1,0:T(8,128)}) custom-call(f32[2]{0:T(128)} %values_ref.1, s32[32,128]{1,0:T(8,128)} %bitcast.14, f32[2,64,256]{2,1,0:T(8,128)} %orb_ref.3, f32[2,64,256]{2,1,0:T(8,128)} %app_ref.1, bf16[640,768]{1,0:T(8,128)(2,1)} %constant.30.clone.up_ref), custom_call_target="tpu_custom_call" | custom-call | flops 2000000000 | bytes 6000000 | tf_op jit(solution)/shard_map/before/pallas_call | solution.py:452
  3.4 10.3 %all-to-all-start = ((f32[64,1,1280]{2,1,0:T(1,128)}), f32[64,1,1280]{2,1,0:T(1,128)S(1)}, u32[]{:S(2)}, u32[]{:S(2)}) async-start(f32[64,1,1280]{2,1,0:T(1,128)} %bitcast.2), calls=%async_computation | async-start | bytes 655360 | tf_op jit(solution)/shard_map/all_to_all | solution.py:436
  13.7 7.5 %prepare.1 = (f32[5,256,256]{2,1,0:T(8,128)S(1)}, s32[512,128]{1,0:T(8,128)S(1)}, s32[32,128]{1,0:T(8,128)}, f32[2,2,64,256]{3,2,1,0:T(8,128)S(1)}, f32[2,2,64,256]{3,2,1,0:T(8,128)S(1)}) custom-call(f32[8,16]{1,0:T(8,128)} %bitcast.17, s32[32,128]{1,0:T(8,128)} %bitcast.15, f32[2,64,256]{2,1,0:T(8,128)} %orb_ref.3, ...), custom_call_target="tpu_custom_call" | custom-call | flops 7000000000 | bytes 21000000 | tf_op jit(solution)/shard_map/prepare/pallas_call | solution.py:452
  21.2 3.3 %collective-permute-start = (f32[2,2,64,256]{3,2,1,0:T(8,128)S(1)}, f32[2,2,64,256]{3,2,1,0:T(8,128)}, u32[]{:S(2)}, u32[]{:S(2)}) collective-permute-start(f32[2,2,64,256]{3,2,1,0:T(8,128)S(1)} %get-tuple-element.19), channel_id=1, source_target_pairs={{0,64},{64,0},{128,192},{192,128},{1,65},{65,1},{129,193},{193,129... | collective-permute-start | bytes 786440 | tf_op jit(solution)/shard_map/ppermute | solution.py:530
  24.5 0.0 all-to-all-done
  24.5 0.0 copy-start
  24.5 0.0 copy-start.1
  24.5 0.0 copy-start.2
  24.5 20.0 %middle.1 = f32[640,128]{1,0:T(8,128)} custom-call(s32[32,128]{1,0:T(8,128)} %get-tuple-element.15.place_hbm, f32[640,128]{1,0:T(8,128)S(1)} %bitcast.12, f32[5,256,256]{2,1,0:T(8,128)S(1)} %get-tuple-element.17.pot_ref, s32[512,128]{1,0:T(8,128)S(1)} %get-tuple-element.18.bits_ref, bf16[512,1024]{1,0:T(8,128)(2,1)} %constant.33.clone.spread_hbm, ...), custom_call_target="tpu_custom_call" | custom-call | flops 20000000000 | bytes 60000000 | tf_op jit(solution)/shard_map/middle/pallas_call | solution.py:452
  44.5 0.0 collective-permute-done
  44.5 9.1 %all-to-all-start.1 = ((f32[64,1,1280]{2,1,0:T(1,128)}), f32[64,1,1280]{2,1,0:T(1,128)S(1)}, u32[]{:S(2)}, u32[]{:S(2)}) async-start(f32[64,1,1280]{2,1,0:T(1,128)} %bitcast.5), calls=%async_computation.1 | async-start | bytes 655360 | tf_op jit(solution)/shard_map/all_to_all | solution.py:436
  53.6 1.0 %add.6 = f32[2,2,64,256]{3,2,1,0:T(8,128)S(1)} add(f32[2,2,64,256]{3,2,1,0:T(8,128)S(1)} %get-tuple-element.14, f32[2,2,64,256]{3,2,1,0:T(8,128)} %collective-permute-done) | non-fusion elementwise | flops 65536 | bytes 786432 | tf_op jit(solution)/shard_map/add | solution.py:533
  54.7 3.4 %collective-permute-start.1 = (f32[2,64,256]{2,1,0:T(8,128)S(1)}, f32[2,64,256]{2,1,0:T(8,128)S(1)}, u32[]{:S(2)}, u32[]{:S(2)}) collective-permute-start(f32[2,64,256]{2,1,0:T(8,128)S(1)} %slice_bitcast_fusion), channel_id=1, source_target_pairs={{0,192},{64,128},{128,64},{192,0},{1,193},{65,129},{129,65},{193,1... | collective-permute-start | bytes 393224 | tf_op jit(solution)/shard_map/ppermute | solution.py:534
  58.0 6.1 %all-to-all-done.1 = f32[64,1,1280]{2,1,0:T(1,128)S(1)} async-done(((f32[64,1,1280]{2,1,0:T(1,128)}), f32[64,1,1280]{2,1,0:T(1,128)S(1)}, u32[]{:S(2)}, u32[]{:S(2)}) %all-to-all-start.1) | async-done | bytes 327712 | tf_op jit(solution)/shard_map/all_to_all | solution.py:436
  64.1 0.0 copy-done
  64.1 0.0 copy-done.1
  64.1 0.0 copy-done.2
  64.1 1.2 %after.1 = f32[2,64,256]{2,1,0:T(8,128)} custom-call(s32[32,128]{1,0:T(8,128)S(1)} %bitcast.16, f32[2,64,256]{2,1,0:T(8,128)S(1)} %copy-done.2, f32[640,128]{1,0:T(8,128)S(1)} %bitcast.13, bf16[256,1920]{1,0:T(8,128)(2,1)S(1)} %copy-done.1), custom_call_target="tpu_custom_call" | custom-call | flops 2000000000 | bytes 6000000 | tf_op jit(solution)/shard_map/after/pallas_call | solution.py:452
  65.3 0.0 collective-permute-done.1
  65.3 0.7 %fusion = f32[2,64,256]{2,1,0:T(8,128)} fusion(f32[2,64,256]{2,1,0:T(8,128)S(1)} %collective-permute-done.1, f32[2,2,64,256]{3,2,1,0:T(8,128)S(1)} %add.6), kind=kLoop, calls=%fused_computation.2 | loop fusion | flops 32768 | bytes 393216 | tf_op jit(solution)/shard_map/add | solution.py:545
  (1 shorter events, 0.0 us)
Async XLA Ops:
  3.4 21.1 %all-to-all-start = ((f32[64,1,1280]{2,1,0:T(1,128)}), f32[64,1,1280]{2,1,0:T(1,128)S(1)}, u32[]{:S(2)}, u32[]{:S(2)}) async-start(f32[64,1,1280]{2,1,0:T(1,128)} %bitcast.2), calls=%async_computation | async-start | bytes 655360 | tf_op jit(solution)/shard_map/all_to_all | solution.py:436
  21.2 23.3 %collective-permute-start = (f32[2,2,64,256]{3,2,1,0:T(8,128)S(1)}, f32[2,2,64,256]{3,2,1,0:T(8,128)}, u32[]{:S(2)}, u32[]{:S(2)}) collective-permute-start(f32[2,2,64,256]{3,2,1,0:T(8,128)S(1)} %get-tuple-element.19), channel_id=1, source_target_pairs={{0,64},{64,0},{128,192},{192,128},{1,65},{65,1},{129,193},{193,129... | collective-permute-start | bytes 786440 | tf_op jit(solution)/shard_map/ppermute | solution.py:530
  24.5 39.6 %copy-start = (s32[4096]{0:T(1024)S(1)}, s32[4096]{0:T(1024)}, u32[]{:S(2)}) copy-start(s32[4096]{0:T(1024)} %param.21) | copy-start | bytes 49156
  24.5 39.6 %copy-start.1 = (bf16[256,1920]{1,0:T(8,128)(2,1)S(1)}, bf16[256,1920]{1,0:T(8,128)(2,1)}, u32[]{:S(2)}) copy-start(bf16[256,1920]{1,0:T(8,128)(2,1)} %constant.31.clone.down_ref) | copy-start | bytes 2949124
  24.5 39.6 %copy-start.2 = (f32[2,64,256]{2,1,0:T(8,128)S(1)}, f32[2,64,256]{2,1,0:T(8,128)}, u32[]{:S(2)}) copy-start(f32[2,64,256]{2,1,0:T(8,128)} %get-tuple-element.13.corr_ref) | copy-start | bytes 393220
  44.5 19.6 %all-to-all-start.1 = ((f32[64,1,1280]{2,1,0:T(1,128)}), f32[64,1,1280]{2,1,0:T(1,128)S(1)}, u32[]{:S(2)}, u32[]{:S(2)}) async-start(f32[64,1,1280]{2,1,0:T(1,128)} %bitcast.5), calls=%async_computation.1 | async-start | bytes 655360 | tf_op jit(solution)/shard_map/all_to_all | solution.py:436
  54.7 10.6 %collective-permute-start.1 = (f32[2,64,256]{2,1,0:T(8,128)S(1)}, f32[2,64,256]{2,1,0:T(8,128)S(1)}, u32[]{:S(2)}, u32[]{:S(2)}) collective-permute-start(f32[2,64,256]{2,1,0:T(8,128)S(1)} %slice_bitcast_fusion), channel_id=1, source_target_pairs={{0,192},{64,128},{128,64},{192,0},{1,193},{65,129},{129,65},{193,1... | collective-permute-start | bytes 393224 | tf_op jit(solution)/shard_map/ppermute | solution.py:534

commit v3 on v2

--- a/solution.py
+++ b/solution.py
@@ -125,12 +125,19 @@
     return dict(
         **folded_tables(),
         row_down=three([high.T, high.T, low.T], 0),
-        stick_up=three([s_high.T, s_low.T, s_high.T], 1),
+        stick_up=three([s_high.T, s_low.T], 1),
         stick_down=three([s_high, s_low, s_high], 1),
-        fine_cols=three([r_high, r_low, r_high], 1),
+        fine_cols=three([r_high, r_low, r_high, np.zeros((FINE, 64), r_high.dtype)], 1),
         spread=spreading_table(),
         choose=choosing_table(),
-        fine_rows=np.stack([r_high.T, r_low.T]),
+        fine_rows=three(
+            [
+                *(r.T[:FINE] for r in (r_high, r_high, r_low)),
+                *(r.T[FINE:] for r in (r_high, r_high, r_low)),
+                np.zeros((64, FINE), r_high.dtype),
+            ],
+            0,
+        ),
     )
 
 
@@ -191,7 +198,23 @@
     return (planar + (fz * fz).astype(F32)) * (1.0 / (WIDTH // 2) ** 2)
 
 
-def before_kernel(values_ref, map_ref, orb_ref, app_ref, up_ref, send_ref, corr_ref):
+def before_kernel(
+    values_hbm, map_hbm, orb_hbm, app_hbm, up_hbm, send_ref, corr_hbm,
+    values_ref, map_ref, orb_ref, app_ref, up_ref, corr_ref, sems,
+):
+    pairs = (
+        (values_hbm, values_ref),
+        (map_hbm, map_ref),
+        (orb_hbm, orb_ref),
+        (app_hbm, app_ref),
+        (up_hbm, up_ref),
+        (corr_ref, corr_hbm),
+    )
+    copies = [pltpu.make_async_copy(source, target, sems.at[i]) for i, (source, target) in enumerate(pairs)]
+    for copy in copies[:5]:
+        copy.start()
+    for copy in copies[:4]:
+        copy.wait()
     sticks = orb_ref.shape[1]
     kinetic = kinetic_of(map_ref, sticks)
     scale = 1.0 + jnp.concatenate([kinetic, kinetic], 1)
@@ -200,20 +223,37 @@
         c = (app_ref[b] - values_ref[b] * orb_ref[b]) / scale
         corr_ref[b] = c
         corr.append(c)
+    copies[5].start()
     rows = jnp.concatenate(corr, 0)
     turned = jnp.concatenate([rows[:, :128].T, rows[:, 128:].T], 0)
-    send_ref[...] = dot(up_ref[...], data_rows(turned, 0))
+    high, low = halves(turned)
+    copies[4].wait()
+    both = jnp.concatenate([high, high], 0)
+    for at in range(0, GROUP * PARTS, 160):
+        send_ref[at : at + 160, :] = dot(up_ref[at : at + 160, :], both) + dot(up_ref[at : at + 160, : 2 * WIDTH], low)
+    copies[5].wait()
 
 
 def prepare_kernel(
-    rotation_ref, map_ref, orb_ref, corr_ref, pot_hbm, rows_ref, cols_ref, out_ref, bits_ref, place_ref, keep_ref, pass_ref,
-    pot_ref, work_ref, sems,
+    rotation_hbm, map_hbm, orb_hbm, corr_hbm, pot_hbm, rows_hbm, cols_hbm, out_ref, bits_ref, place_ref, keep_ref, pass_ref,
+    rotation_ref, map_ref, orb_ref, corr_ref, pot_ref, rows_ref, cols_ref, work_ref, sems,
 ):
-    copies = [
-        pltpu.make_async_copy(pot_hbm.at[p], pot_ref.at[pl.ds(p * LENGTH, LENGTH), :], sems.at[p]) for p in range(PLANES)
+    pairs = [
+        (rotation_hbm, rotation_ref),
+        (map_hbm, map_ref),
+        (orb_hbm, orb_ref),
+        (corr_hbm, corr_ref),
+        (rows_hbm, rows_ref),
+        *((pot_hbm.at[p], pot_ref.at[p]) for p in range(PLANES)),
+        (cols_hbm, cols_ref),
     ]
+    copies = [pltpu.make_async_copy(source, target, sems.at[i]) for i, (source, target) in enumerate(pairs)]
     for copy in copies:
         copy.start()
+    for p in range(PLANES):
+        work_ref[p, 3 * LENGTH :] = jnp.zeros((64, FINE), BF16)
+    for copy in copies[:4]:
+        copy.wait()
     me = lax.axis_index("bg")
     all_bands = rotation_ref.shape[0]
     for target, group in ((keep_ref, me), (pass_ref, me ^ 1)):
@@ -233,36 +273,36 @@
     stick = lax.broadcasted_iota(jnp.int32, (16, 128), 1)
     eight = lax.broadcasted_iota(jnp.int32, (16, 128), 0)
     weights = jnp.where((stick >> 3) == eight, (1 << (stick & 7)).astype(F32), 0.0).astype(BF16)
-    rows_high, rows_low = rows_ref[0], rows_ref[1]
-    marked = arrived = done = 0
-    for at in range(0, PLANES * LENGTH, 256):
-        end = min(at + 256, PLANES * LENGTH)
-        while arrived * LENGTH < end:
-            copies[arrived].wait()
-            arrived += 1
-        high, low = halves(pot_ref[at:end, :])
-        part = dot(high, rows_high) + (dot(low, rows_high) + dot(high, rows_low))
-        high, low = halves(part)
-        for p in range(at // LENGTH, (end - 1) // LENGTH + 1):
-            first, stop = max(at, p * LENGTH), min(end, (p + 1) * LENGTH)
+    marked = 0
+    copies[4].wait()
+    for p in range(PLANES):
+        copies[5 + p].wait()
+        for at in range(0, LENGTH, LENGTH // 2):
+            end = at + LENGTH // 2
+            high, low = halves(pot_ref[p, at:end, :FINE])
+            rest = pot_ref[p, at:end, FINE:]
+            rest_high = rest.astype(BF16).astype(F32)
+            rest = jnp.concatenate([rest_high, rest - rest_high, rest_high, jnp.zeros_like(rest)], 1)
+            part = dot(jnp.concatenate([high, low, high, rest.astype(BF16)], 1), rows_ref[...])
+            high, low = halves(part)
             for k, values in enumerate((high, high, low)):
-                to = k * LENGTH + first - p * LENGTH
-                work_ref[p, to : to + stop - first] = values[first - at : stop - at]
-        while (done + 1) * LENGTH <= end:
-            out_ref[done] = dot(cols_ref[...], work_ref[done])
-            done += 1
-        while marked < STICKS // 128 and marked < (at // 256 + 1) * 5:
-            match = jnp.where(columns[marked : marked + 1, :] == row_block, 1.0, 0.0).astype(BF16)
-            bits = lax.dot_general(weights, match, (((1,), (1,)), ((), ())), preferred_element_type=F32)
-            bits_ref[marked * 16 : marked * 16 + 16, :] = bits.astype(jnp.int32)
-            marked += 1
+                work_ref[p, k * LENGTH + at : k * LENGTH + end] = values
+            for _ in range(4):
+                if marked < STICKS // 128:
+                    match = jnp.where(columns[marked : marked + 1, :] == row_block, 1.0, 0.0).astype(BF16)
+                    bits = lax.dot_general(weights, match, (((1,), (1,)), ((), ())), preferred_element_type=F32)
+                    bits_ref[marked * 16 : marked * 16 + 16, :] = bits.astype(jnp.int32)
+                    marked += 1
+        if p == 0:
+            copies[5 + PLANES].wait()
+        out_ref[p] = dot(cols_ref[...], work_ref[p])
 
 
 def middle_kernel(
     place_hbm, recv_ref, pot_ref, bits_ref, spread_hbm, row_up_hbm, even_up_hbm, odd_up_hbm, even_down_hbm,
     odd_down_hbm, row_down_hbm, choose_hbm,
-    send_ref,
-    place_ref, sticks_ref, square_ref, turned_ref, rows_ref, half_ref, back_ref,
+    send_hbm,
+    send_ref, place_ref, sticks_ref, square_ref, turned_ref, rows_ref, half_ref, back_ref,
     spread, row_up, even_up, odd_up, even_down, odd_down, row_down, choose, sems,
 ):
     copies = [
@@ -396,6 +436,7 @@
         return 0
 
     lax.fori_loop(0, STICKS // 128, gather, 0)
+    sent = []
     own_bit = 1 << (lax.broadcasted_iota(jnp.int32, (256, 128), 0) & 7)
     for at in range(0, STICKS, 256):
         bits = jnp.broadcast_to(bits_ref[at // 8 : at // 8 + 32, :][:, None, :], (32, 8, 128)).reshape(256, 128)
@@ -415,6 +456,12 @@
                 to = (at // 64 + 2 * h + i) * PARTS
                 send_ref[to : to + PLANES, :] = part[:PLANES]
                 send_ref[to + PLANES : to + PARTS, :] = part[8 : 8 + PLANES]
+        if at % 1024 == 768:
+            part = pl.ds((at - 768) // 64 * PARTS, 16 * PARTS)
+            sent.append(pltpu.make_async_copy(send_ref.at[part, :], send_hbm.at[part, :], sems.at[9 + len(sent)]))
+            sent[-1].start()
+    for copy in sent:
+        copy.wait()
 
 
 def after_kernel(map_ref, corr_ref, recv_ref, down_ref, out_ref):
@@ -469,10 +516,11 @@
         "middle",
         20,
         (in_hbm(place), in_vmem(received), in_vmem(local), in_vmem(mask), *(in_hbm(t[n]) for n in names)),
-        pltpu.VMEM((GROUP * PARTS, 128), F32),
+        pltpu.HBM((GROUP * PARTS, 128), F32),
         [ANY, VMEM, VMEM, VMEM] + [ANY] * 8,
-        VMEM,
+        ANY,
         [
+            pltpu.VMEM((GROUP * PARTS, 128), F32),
             pltpu.SMEM((STICKS // 128, 128), jnp.int32),
             pltpu.VMEM((STICKS, 128), F32),
             pltpu.VMEM((STICKS, 128), F32),
@@ -481,7 +529,7 @@
             pltpu.VMEM((grid, 2 * FINE), F32),
             pltpu.VMEM((grid, FINE), F32),
             *(pltpu.VMEM(t[n].shape, BF16) for n in names),
-            pltpu.SemaphoreType.DMA((9,)),
+            pltpu.SemaphoreType.DMA((13,)),
         ],
     )
 
@@ -503,12 +551,18 @@
             pltpu.VMEM((2, BANDS, sticks, doubled), F32),
             pltpu.VMEM((2, BANDS, sticks, doubled), F32),
         ),
-        [SMEM, VMEM, VMEM, VMEM, ANY, VMEM, VMEM],
+        [ANY] * 7,
         (VMEM,) * 5,
         [
-            pltpu.VMEM((PLANES * LENGTH, LENGTH), F32),
-            pltpu.VMEM((PLANES, 3 * LENGTH, FINE), BF16),
-            pltpu.SemaphoreType.DMA((PLANES,)),
+            pltpu.SMEM(rotation.shape, F32),
+            pltpu.VMEM(map_rows.shape, jnp.int32),
+            pltpu.VMEM(orbitals.shape, F32),
+            pltpu.VMEM(orbitals.shape, F32),
+            pltpu.VMEM((PLANES, LENGTH, LENGTH), F32),
+            pltpu.VMEM(t["fine_rows"].shape, BF16),
+            pltpu.VMEM(t["fine_cols"].shape, BF16),
+            pltpu.VMEM((PLANES, 3 * LENGTH + 64, FINE), BF16),
+            pltpu.SemaphoreType.DMA((PLANES + 6,)),
         ],
     )
 
@@ -522,8 +576,17 @@
         2,
         tuple(in_hbm(x) for x in (ritz_values, map_rows, orbitals, applied_orbitals, t["stick_up"])),
         (pltpu.VMEM((GROUP * PARTS, 128), F32), pltpu.HBM(orbitals.shape, F32)),
-        [SMEM] + [VMEM] * 4,
-        (VMEM, VMEM),
+        [ANY] * 5,
+        (VMEM, ANY),
+        [
+            pltpu.SMEM(ritz_values.shape, F32),
+            pltpu.VMEM(map_rows.shape, jnp.int32),
+            pltpu.VMEM(orbitals.shape, F32),
+            pltpu.VMEM(orbitals.shape, F32),
+            pltpu.VMEM(t["stick_up"].shape, BF16),
+            pltpu.VMEM(orbitals.shape, F32),
+            pltpu.SemaphoreType.DMA((6,)),
+        ],
     )
     received = exchange(sent)
     local, mask, place, kept, passed = prepare(ritz_rotation.T, map_rows, orbitals, correction, potential, t)

time: 66.3 us -> 64.9 us (0.979)
  Pallas kernels: 31.4 us -> 29.9 us
  waiting for transfers between devices: 6.08 us -> 6.99 us
  starting transfers between devices: 26.1 us -> 25.2 us
    pallas_call x4, Pallas kernels: 31.4 us -> 29.9 us  [call(): pl.pallas_call(kernel, out_shape=out_shape, in_specs=in_specs, out_specs=...]
    all_to_all x2, waiting for transfers between devices: 6.08 us -> 6.98 us  [exchange(): lax.all_to_all(values, 'pw', 0, 0, tiled=True).reshape(GROUP * PARTS, 128)]
    all_to_all x2, starting transfers between devices: 19.5 us -> 18.6 us  [exchange(): lax.all_to_all(values, 'pw', 0, 0, tiled=True).reshape(GROUP * PARTS, 128)]
  transfers between devices with their start and end apart: 4 -> 4, of which waited for: 1 -> 2; matrix products, arithmetic and copies ran while one was open for 2% -> 2% of each run, Pallas kernels for 43% -> 42%
where the time goes in v3:
time: 64.9 us; the launch traced here: 64.5 us
  Pallas kernels  29.9 us (46%)
  starting transfers between devices  25.2 us (39%)
  waiting for transfers between devices  6.99 us (11%)
  other arithmetic  1.66 us (3%)
  between operations  0.7 us (1%)
    pallas_call x4, Pallas kernels, call(): pl.pallas_call(kernel, out_shape=out_shape, in_specs=in_specs, out_specs=...  29.9 us
    all_to_all x2, starting transfers between devices, exchange(): lax.all_to_all(values, 'pw', 0, 0, tiled=True).reshape(GROUP * PARTS, 128)  18.6 us
    all_to_all x2, waiting for transfers between devices, exchange(): lax.all_to_all(values, 'pw', 0, 0, tiled=True).reshape(GROUP * PARTS, 128)  6.98 us
    ppermute x1, starting transfers between devices, on_device(): last = lax.ppermute(halved[1], 'bg', [(i, 3 - i) for i in range(4)])  3.39 us
    ppermute x1, starting transfers between devices, on_device(): came = lax.ppermute(passed, 'bg', [(i, i ^ 1) for i in range(4)])  3.25 us
  transfers between devices with their start and end apart: 4, of which 2 were waited for; matrix products, arithmetic and copies ran while one was open for 2% of the time, Pallas kernels for 42%

profile of v3, /device:TPU:1, one launch (start us, length us, event | category | flops | bytes accessed | tf_op | source)
XLA Modules:
  0.0 64.5 jit_solution(2602870540245794513)
XLA Ops:
  0.6 2.5 %before.1 = (f32[640,128]{1,0:T(8,128)}, f32[2,64,256]{2,1,0:T(8,128)}) custom-call(f32[2]{0:T(128)} %values_hbm.1, s32[32,128]{1,0:T(8,128)} %bitcast.14, f32[2,64,256]{2,1,0:T(8,128)} %orb_hbm.3, f32[2,64,256]{2,1,0:T(8,128)} %app_hbm.1, bf16[640,512]{1,0:T(8,128)(2,1)} %constant.30.clone.up_hbm), custom_call_target="tpu_custom_call" | custom-call | flops 2000000000 | bytes 6000000 | tf_op jit(solution)/shard_map/before/pallas_call | solution.py:499
  3.2 10.4 %all-to-all-start = ((f32[64,1,1280]{2,1,0:T(1,128)}), f32[64,1,1280]{2,1,0:T(1,128)S(1)}, u32[]{:S(2)}, u32[]{:S(2)}) async-start(f32[64,1,1280]{2,1,0:T(1,128)} %bitcast.2), calls=%async_computation | async-start | bytes 655360 | tf_op jit(solution)/shard_map/all_to_all | solution.py:483
  13.5 6.3 %prepare.1 = (f32[5,256,256]{2,1,0:T(8,128)S(1)}, s32[512,128]{1,0:T(8,128)S(1)}, s32[32,128]{1,0:T(8,128)}, f32[2,2,64,256]{3,2,1,0:T(8,128)S(1)}, f32[2,2,64,256]{3,2,1,0:T(8,128)S(1)}) custom-call(f32[8,16]{1,0:T(8,128)} %bitcast.18, s32[32,128]{1,0:T(8,128)} %bitcast.15, f32[2,64,256]{2,1,0:T(8,128)} %orb_hbm.3, ...), custom_call_target="tpu_custom_call" | custom-call | flops 7000000000 | bytes 21000000 | tf_op jit(solution)/shard_map/prepare/pallas_call | solution.py:499
  19.9 3.3 %collective-permute-start = (f32[2,2,64,256]{3,2,1,0:T(8,128)S(1)}, f32[2,2,64,256]{3,2,1,0:T(8,128)}, u32[]{:S(2)}, u32[]{:S(2)}) collective-permute-start(f32[2,2,64,256]{3,2,1,0:T(8,128)S(1)} %get-tuple-element.19), channel_id=1, source_target_pairs={{0,64},{64,0},{128,192},{192,128},{1,65},{65,1},{129,193},{193,129... | collective-permute-start | bytes 786440 | tf_op jit(solution)/shard_map/ppermute | solution.py:593
  23.1 0.9 %all-to-all-done = f32[64,1,1280]{2,1,0:T(1,128)S(1)} async-done(((f32[64,1,1280]{2,1,0:T(1,128)}), f32[64,1,1280]{2,1,0:T(1,128)S(1)}, u32[]{:S(2)}, u32[]{:S(2)}) %all-to-all-start) | async-done | bytes 327712 | tf_op jit(solution)/shard_map/all_to_all | solution.py:483
  24.0 0.0 copy-start
  24.0 0.0 copy-start.1
  24.0 0.0 copy-start.2
  24.0 19.9 %middle.1 = f32[640,128]{1,0:T(8,128)} custom-call(s32[32,128]{1,0:T(8,128)} %get-tuple-element.15.place_hbm, f32[640,128]{1,0:T(8,128)S(1)} %bitcast.12, f32[5,256,256]{2,1,0:T(8,128)S(1)} %get-tuple-element.17.pot_ref, s32[512,128]{1,0:T(8,128)S(1)} %get-tuple-element.18.bits_ref, bf16[512,1024]{1,0:T(8,128)(2,1)} %constant.33.clone.spread_hbm, ...), custom_call_target="tpu_custom_call" | custom-call | flops 20000000000 | bytes 60000000 | tf_op jit(solution)/shard_map/middle/pallas_call | solution.py:499
  43.9 0.0 collective-permute-done
  44.0 8.2 %all-to-all-start.1 = ((f32[64,1,1280]{2,1,0:T(1,128)}), f32[64,1,1280]{2,1,0:T(1,128)S(1)}, u32[]{:S(2)}, u32[]{:S(2)}) async-start(f32[64,1,1280]{2,1,0:T(1,128)} %bitcast.17), calls=%async_computation.1 | async-start | bytes 655360 | tf_op jit(solution)/shard_map/all_to_all | solution.py:483
  52.2 1.0 %add.6 = f32[2,2,64,256]{3,2,1,0:T(8,128)S(1)} add(f32[2,2,64,256]{3,2,1,0:T(8,128)S(1)} %get-tuple-element.14, f32[2,2,64,256]{3,2,1,0:T(8,128)} %collective-permute-done) | non-fusion elementwise | flops 65536 | bytes 786432 | tf_op jit(solution)/shard_map/add | solution.py:596
  53.2 3.4 %collective-permute-start.1 = (f32[2,64,256]{2,1,0:T(8,128)S(1)}, f32[2,64,256]{2,1,0:T(8,128)S(1)}, u32[]{:S(2)}, u32[]{:S(2)}) collective-permute-start(f32[2,64,256]{2,1,0:T(8,128)S(1)} %slice_bitcast_fusion), channel_id=1, source_target_pairs={{0,192},{64,128},{128,64},{192,0},{1,193},{65,129},{129,65},{193,1... | collective-permute-start | bytes 393224 | tf_op jit(solution)/shard_map/ppermute | solution.py:597
  56.6 6.1 %all-to-all-done.1 = f32[64,1,1280]{2,1,0:T(1,128)S(1)} async-done(((f32[64,1,1280]{2,1,0:T(1,128)}), f32[64,1,1280]{2,1,0:T(1,128)S(1)}, u32[]{:S(2)}, u32[]{:S(2)}) %all-to-all-start.1) | async-done | bytes 327712 | tf_op jit(solution)/shard_map/all_to_all | solution.py:483
  62.7 0.0 copy-done
  62.7 0.0 copy-done.1
  62.7 0.0 copy-done.2
  62.7 1.2 %after.1 = f32[2,64,256]{2,1,0:T(8,128)} custom-call(s32[32,128]{1,0:T(8,128)S(1)} %bitcast.16, f32[2,64,256]{2,1,0:T(8,128)S(1)} %copy-done.2, f32[640,128]{1,0:T(8,128)S(1)} %bitcast.13, bf16[256,1920]{1,0:T(8,128)(2,1)S(1)} %copy-done.1), custom_call_target="tpu_custom_call" | custom-call | flops 2000000000 | bytes 6000000 | tf_op jit(solution)/shard_map/after/pallas_call | solution.py:499
  63.9 0.0 collective-permute-done.1
  63.9 0.7 %fusion = f32[2,64,256]{2,1,0:T(8,128)} fusion(f32[2,64,256]{2,1,0:T(8,128)S(1)} %collective-permute-done.1, f32[2,2,64,256]{3,2,1,0:T(8,128)S(1)} %add.6), kind=kLoop, calls=%fused_computation.2 | loop fusion | flops 32768 | bytes 393216 | tf_op jit(solution)/shard_map/add | solution.py:608
  (1 shorter events, 0.0 us)
Async XLA Ops:
  3.2 20.8 %all-to-all-start = ((f32[64,1,1280]{2,1,0:T(1,128)}), f32[64,1,1280]{2,1,0:T(1,128)S(1)}, u32[]{:S(2)}, u32[]{:S(2)}) async-start(f32[64,1,1280]{2,1,0:T(1,128)} %bitcast.2), calls=%async_computation | async-start | bytes 655360 | tf_op jit(solution)/shard_map/all_to_all | solution.py:483
  19.9 24.1 %collective-permute-start = (f32[2,2,64,256]{3,2,1,0:T(8,128)S(1)}, f32[2,2,64,256]{3,2,1,0:T(8,128)}, u32[]{:S(2)}, u32[]{:S(2)}) collective-permute-start(f32[2,2,64,256]{3,2,1,0:T(8,128)S(1)} %get-tuple-element.19), channel_id=1, source_target_pairs={{0,64},{64,0},{128,192},{192,128},{1,65},{65,1},{129,193},{193,129... | collective-permute-start | bytes 786440 | tf_op jit(solution)/shard_map/ppermute | solution.py:593
  24.0 38.7 %copy-start = (s32[4096]{0:T(1024)S(1)}, s32[4096]{0:T(1024)}, u32[]{:S(2)}) copy-start(s32[4096]{0:T(1024)} %param.21) | copy-start | bytes 49156
  24.0 38.7 %copy-start.1 = (bf16[256,1920]{1,0:T(8,128)(2,1)S(1)}, bf16[256,1920]{1,0:T(8,128)(2,1)}, u32[]{:S(2)}) copy-start(bf16[256,1920]{1,0:T(8,128)(2,1)} %constant.31.clone.down_ref) | copy-start | bytes 2949124
  24.0 38.7 %copy-start.2 = (f32[2,64,256]{2,1,0:T(8,128)S(1)}, f32[2,64,256]{2,1,0:T(8,128)}, u32[]{:S(2)}) copy-start(f32[2,64,256]{2,1,0:T(8,128)} %get-tuple-element.13.corr_hbm.corr_ref) | copy-start | bytes 393220
  44.0 18.7 %all-to-all-start.1 = ((f32[64,1,1280]{2,1,0:T(1,128)}), f32[64,1,1280]{2,1,0:T(1,128)S(1)}, u32[]{:S(2)}, u32[]{:S(2)}) async-start(f32[64,1,1280]{2,1,0:T(1,128)} %bitcast.17), calls=%async_computation.1 | async-start | bytes 655360 | tf_op jit(solution)/shard_map/all_to_all | solution.py:483
  53.2 10.6 %collective-permute-start.1 = (f32[2,64,256]{2,1,0:T(8,128)S(1)}, f32[2,64,256]{2,1,0:T(8,128)S(1)}, u32[]{:S(2)}, u32[]{:S(2)}) collective-permute-start(f32[2,64,256]{2,1,0:T(8,128)S(1)} %slice_bitcast_fusion), channel_id=1, source_target_pairs={{0,192},{64,128},{128,64},{192,0},{1,193},{65,129},{129,65},{193,1... | collective-permute-start | bytes 393224 | tf_op jit(solution)/shard_map/ppermute | solution.py:597

commit v4 on v3

--- a/solution.py
+++ b/solution.py
@@ -107,14 +107,6 @@
     return table.reshape(512, 1024).astype(ml_dtypes.bfloat16)
 
 
-def choosing_table():
-    table = np.zeros((2, 16, 2, 4, 2, 16))
-    for b in range(2):
-        for part in range(16):
-            table[b, part, :, :, b, part] = 1.0
-    return table.reshape(32, 256).astype(ml_dtypes.bfloat16)
-
-
 def tables():
     high, low = split_host(complex_table(frequency_slots(), point_slots(), FINE))
     stick = complex_table(np.arange(WIDTH) - HALF, np.arange(LENGTH), LENGTH).reshape(2 * WIDTH, 2, GROUP, PLANES)
@@ -129,7 +121,7 @@
         stick_down=three([s_high, s_low, s_high], 1),
         fine_cols=three([r_high, r_low, r_high, np.zeros((FINE, 64), r_high.dtype)], 1),
         spread=spreading_table(),
-        choose=choosing_table(),
+        same=np.tile(np.eye(128), (1, 2)).astype(ml_dtypes.bfloat16),
         fine_rows=three(
             [
                 *(r.T[:FINE] for r in (r_high, r_high, r_low)),
@@ -235,7 +227,7 @@
 
 
 def prepare_kernel(
-    rotation_hbm, map_hbm, orb_hbm, corr_hbm, pot_hbm, rows_hbm, cols_hbm, out_ref, bits_ref, place_ref, keep_ref, pass_ref,
+    rotation_hbm, map_hbm, orb_hbm, corr_hbm, pot_hbm, rows_hbm, cols_hbm, out_ref, bits_ref, block_ref, place_ref, keep_ref, pass_ref,
     rotation_ref, map_ref, orb_ref, corr_ref, pot_ref, rows_ref, cols_ref, work_ref, sems,
 ):
     pairs = [
@@ -269,6 +261,7 @@
     columns = slot_of(map_ref[...] >> 7)
     place_ref[...] = ((columns >> 2) << 7) | slot_of(map_ref[...] & 127)
     columns = columns & 3
+    block_ref[...] = columns
     row_block = lax.broadcasted_iota(jnp.int32, (128, 128), 0) >> 5
     stick = lax.broadcasted_iota(jnp.int32, (16, 128), 1)
     eight = lax.broadcasted_iota(jnp.int32, (16, 128), 0)
@@ -298,12 +291,17 @@
         out_ref[p] = dot(cols_ref[...], work_ref[p])
 
 
+def across(same, x):
+    both = jnp.concatenate(halves(x), 1)
+    return lax.dot_general(same[...], both, (((1,), (1,)), ((), ())), preferred_element_type=F32)
+
+
 def middle_kernel(
-    place_hbm, recv_ref, pot_ref, bits_ref, spread_hbm, row_up_hbm, even_up_hbm, odd_up_hbm, even_down_hbm,
-    odd_down_hbm, row_down_hbm, choose_hbm,
+    place_hbm, recv_ref, pot_ref, bits_ref, block_hbm, spread_hbm, row_up_hbm, even_up_hbm, odd_up_hbm, even_down_hbm,
+    odd_down_hbm, row_down_hbm, same_hbm,
     send_hbm,
-    send_ref, place_ref, sticks_ref, square_ref, turned_ref, rows_ref, half_ref, back_ref,
-    spread, row_up, even_up, odd_up, even_down, odd_down, row_down, choose, sems,
+    send_ref, place_ref, block_ref, sticks_ref, square_ref, turned_ref, rows_ref, half_ref, back_ref,
+    spread, row_up, even_up, odd_up, even_down, odd_down, row_down, same, sems,
 ):
     copies = [
         pltpu.make_async_copy(source, target, sems.at[i])
@@ -317,7 +315,8 @@
                 (even_down_hbm, even_down),
                 (odd_down_hbm, odd_down),
                 (row_down_hbm, row_down),
-                (choose_hbm, choose),
+                (same_hbm, same),
+                (block_hbm, block_ref),
             )
         )
     ]
@@ -354,12 +353,8 @@
 
     lax.fori_loop(0, STICKS // 128, scatter, 0)
 
-    def turn(i, _):
-        rows = pl.ds(pl.multiple_of(i * 128, 128), 128)
-        turned_ref[rows, :] = square_ref[rows, :].T
-        return 0
-
-    lax.fori_loop(0, 32, turn, 0, unroll=4)
+    for at in range(0, STICKS, 128):
+        turned_ref[at : at + 128, :] = square_ref[at : at + 128, :].T
     pairs = [(b, p) for b in range(BANDS) for p in range(PLANES)]
     copies[2].wait()
     left = lane < HALF
@@ -422,12 +417,8 @@
                 k * 128 : k * 128 + 128, c * 128 : c * 128 + 128
             ]
 
-    def turn_back(i, _):
-        rows = pl.ds(pl.multiple_of(i * 128, 128), 128)
-        square_ref[rows, :] = turned_ref[rows, :].T
-        return 0
-
-    lax.fori_loop(0, 32, turn_back, 0, unroll=4)
+    for at in range(0, STICKS, 128):
+        square_ref[at : at + 128, :] = turned_ref[at : at + 128, :].T
 
     def gather(i, _):
         first = pl.multiple_of(i * 128, 128)
@@ -437,16 +428,13 @@
 
     lax.fori_loop(0, STICKS // 128, gather, 0)
     sent = []
-    own_bit = 1 << (lax.broadcasted_iota(jnp.int32, (256, 128), 0) & 7)
+    left = lane < 64
     for at in range(0, STICKS, 256):
-        bits = jnp.broadcast_to(bits_ref[at // 8 : at // 8 + 32, :][:, None, :], (32, 8, 128)).reshape(256, 128)
-        rows = jnp.where((bits & own_bit) != 0, sticks_ref[at : at + 256, :], 0.0)
-        found = lax.dot_general(
-            choose[...],
-            jnp.concatenate(halves(rows), 1),
-            (((1,), (1,)), ((), ())),
-            preferred_element_type=F32,
-        )
+        every = across(same, sticks_ref[at : at + 256, :])
+        own = jnp.concatenate([block_ref[at // 128 + i : at // 128 + i + 1, :] for i in range(2)], 1)
+        found = every[:32]
+        for h in range(1, 4):
+            found = jnp.where(own == h, every[32 * h : 32 * h + 32], found)
         for h in range(2):
             here = found[:, h * 128 : h * 128 + 128]
             swapped = pltpu.roll(here, 64, 1)
@@ -458,7 +446,7 @@
                 send_ref[to + PLANES : to + PARTS, :] = part[8 : 8 + PLANES]
         if at % 1024 == 768:
             part = pl.ds((at - 768) // 64 * PARTS, 16 * PARTS)
-            sent.append(pltpu.make_async_copy(send_ref.at[part, :], send_hbm.at[part, :], sems.at[9 + len(sent)]))
+            sent.append(pltpu.make_async_copy(send_ref.at[part, :], send_hbm.at[part, :], sems.at[10 + len(sent)]))
             sent[-1].start()
     for copy in sent:
         copy.wait()
@@ -508,20 +496,21 @@
     )(*inputs)
 
 
-def middle(place, received, local, mask, t):
+def middle(place, received, local, bits, block, t):
     grid = BANDS * PLANES * 128
-    names = ("spread", "row_up", "even_up", "odd_up", "even_down", "odd_down", "row_down", "choose")
+    names = ("spread", "row_up", "even_up", "odd_up", "even_down", "odd_down", "row_down", "same")
     return call(
         middle_kernel,
         "middle",
         20,
-        (in_hbm(place), in_vmem(received), in_vmem(local), in_vmem(mask), *(in_hbm(t[n]) for n in names)),
+        (in_hbm(place), in_vmem(received), in_vmem(local), in_vmem(bits), in_hbm(block), *(in_hbm(t[n]) for n in names)),
         pltpu.HBM((GROUP * PARTS, 128), F32),
-        [ANY, VMEM, VMEM, VMEM] + [ANY] * 8,
+        [ANY] + [VMEM] * 3 + [ANY] * 9,
         ANY,
         [
             pltpu.VMEM((GROUP * PARTS, 128), F32),
             pltpu.SMEM((STICKS // 128, 128), jnp.int32),
+            pltpu.VMEM((STICKS // 128, 128), jnp.int32),
             pltpu.VMEM((STICKS, 128), F32),
             pltpu.VMEM((STICKS, 128), F32),
             pltpu.VMEM((STICKS, 128), F32),
@@ -529,7 +518,7 @@
             pltpu.VMEM((grid, 2 * FINE), F32),
             pltpu.VMEM((grid, FINE), F32),
             *(pltpu.VMEM(t[n].shape, BF16) for n in names),
-            pltpu.SemaphoreType.DMA((13,)),
+            pltpu.SemaphoreType.DMA((14,)),
         ],
     )
 
@@ -548,11 +537,12 @@
             pltpu.VMEM((PLANES, FINE, FINE), F32),
             pltpu.VMEM((STICKS // 8, 128), jnp.int32),
             pltpu.HBM(map_rows.shape, jnp.int32),
+            pltpu.HBM(map_rows.shape, jnp.int32),
             pltpu.VMEM((2, BANDS, sticks, doubled), F32),
             pltpu.VMEM((2, BANDS, sticks, doubled), F32),
         ),
         [ANY] * 7,
-        (VMEM,) * 5,
+        (VMEM,) * 6,
         [
             pltpu.SMEM(rotation.shape, F32),
             pltpu.VMEM(map_rows.shape, jnp.int32),
@@ -589,9 +579,9 @@
         ],
     )
     received = exchange(sent)
-    local, mask, place, kept, passed = prepare(ritz_rotation.T, map_rows, orbitals, correction, potential, t)
+    local, bits, block, place, kept, passed = prepare(ritz_rotation.T, map_rows, orbitals, correction, potential, t)
     came = lax.ppermute(passed, "bg", [(i, i ^ 1) for i in range(4)])
-    product, came = lax.optimization_barrier((middle(place, received, local, mask, t), came))
+    product, came = lax.optimization_barrier((middle(place, received, local, bits, block, t), came))
     returned = exchange(product)
     halved = kept + came
     last = lax.ppermute(halved[1], "bg", [(i, 3 - i) for i in range(4)])

time: 64.9 us -> 63.8 us (0.983)
  Pallas kernels: 29.9 us -> 28.9 us
    pallas_call x4, Pallas kernels: 29.9 us -> 28.9 us  [call(): pl.pallas_call(kernel, out_shape=out_shape, in_specs=in_specs, out_specs=...]
where the time goes in v4:
time: 63.8 us; the launch traced here: 63.5 us
  Pallas kernels  28.9 us (45%)
  starting transfers between devices  25.3 us (40%)
  waiting for transfers between devices  6.98 us (11%)
  other arithmetic  1.66 us (3%)
  between operations  0.7 us (1%)
    pallas_call x4, Pallas kernels, call(): pl.pallas_call(kernel, out_shape=out_shape, in_specs=in_specs, out_specs=...  28.9 us
    all_to_all x2, starting transfers between devices, exchange(): lax.all_to_all(values, 'pw', 0, 0, tiled=True).reshape(GROUP * PARTS, 128)  18.6 us
    all_to_all x2, waiting for transfers between devices, exchange(): lax.all_to_all(values, 'pw', 0, 0, tiled=True).reshape(GROUP * PARTS, 128)  6.98 us
    ppermute x1, starting transfers between devices, on_device(): last = lax.ppermute(halved[1], 'bg', [(i, 3 - i) for i in range(4)])  3.39 us
    ppermute x1, starting transfers between devices, on_device(): came = lax.ppermute(passed, 'bg', [(i, i ^ 1) for i in range(4)])  3.25 us
  transfers between devices with their start and end apart: 4, of which 2 were waited for; matrix products, arithmetic and copies ran while one was open for 2% of the time, Pallas kernels for 42%

profile of v4, /device:TPU:1, one launch (start us, length us, event | category | flops | bytes accessed | tf_op | source)
XLA Modules:
  0.0 63.5 jit_solution(430898161626024015)
XLA Ops:
  0.6 2.5 %before.1 = (f32[640,128]{1,0:T(8,128)}, f32[2,64,256]{2,1,0:T(8,128)}) custom-call(f32[2]{0:T(128)} %values_hbm.1, s32[32,128]{1,0:T(8,128)} %bitcast.14, f32[2,64,256]{2,1,0:T(8,128)} %orb_hbm.3, f32[2,64,256]{2,1,0:T(8,128)} %app_hbm.1, bf16[640,512]{1,0:T(8,128)(2,1)} %constant.30.clone.up_hbm), custom_call_target="tpu_custom_call" | custom-call | flops 2000000000 | bytes 6000000 | tf_op jit(solution)/shard_map/before/pallas_call | solution.py:487
  3.2 10.4 %all-to-all-start = ((f32[64,1,1280]{2,1,0:T(1,128)}), f32[64,1,1280]{2,1,0:T(1,128)S(1)}, u32[]{:S(2)}, u32[]{:S(2)}) async-start(f32[64,1,1280]{2,1,0:T(1,128)} %bitcast.2), calls=%async_computation | async-start | bytes 655360 | tf_op jit(solution)/shard_map/all_to_all | solution.py:471
  13.5 6.3 %prepare.1 = (f32[5,256,256]{2,1,0:T(8,128)S(1)}, s32[512,128]{1,0:T(8,128)S(1)}, s32[32,128]{1,0:T(8,128)}, s32[32,128]{1,0:T(8,128)}, f32[2,2,64,256]{3,2,1,0:T(8,128)S(1)}, /*index=5*/f32[2,2,64,256]{3,2,1,0:T(8,128)S(1)}) custom-call(f32[8,16]{1,0:T(8,128)} %bitcast.18, s32[32,128]{1,0:T(8,128)} %bitcast.15, f32[2,64,256]{2,1,0:T(8,128)} %orb_hbm.3, ...), custom_call_target="tpu_custom_call" | custom-call | flops 7000000000 | bytes 21000000 | tf_op jit(solution)/shard_map/prepare/pallas_call | solution.py:487
  19.9 3.3 %collective-permute-start = (f32[2,2,64,256]{3,2,1,0:T(8,128)S(1)}, f32[2,2,64,256]{3,2,1,0:T(8,128)}, u32[]{:S(2)}, u32[]{:S(2)}) collective-permute-start(f32[2,2,64,256]{3,2,1,0:T(8,128)S(1)} %get-tuple-element.21), channel_id=1, source_target_pairs={{0,64},{64,0},{128,192},{192,128},{1,65},{65,1},{129,193},{193,129... | collective-permute-start | bytes 786440 | tf_op jit(solution)/shard_map/ppermute | solution.py:583
  23.1 0.9 %all-to-all-done = f32[64,1,1280]{2,1,0:T(1,128)S(1)} async-done(((f32[64,1,1280]{2,1,0:T(1,128)}), f32[64,1,1280]{2,1,0:T(1,128)S(1)}, u32[]{:S(2)}, u32[]{:S(2)}) %all-to-all-start) | async-done | bytes 327712 | tf_op jit(solution)/shard_map/all_to_all | solution.py:471
  24.0 0.0 copy-start
  24.0 0.0 copy-start.1
  24.0 0.0 copy-start.2
  24.0 18.9 %middle.1 = f32[640,128]{1,0:T(8,128)} custom-call(s32[32,128]{1,0:T(8,128)} %get-tuple-element.16.place_hbm, f32[640,128]{1,0:T(8,128)S(1)} %bitcast.12, f32[5,256,256]{2,1,0:T(8,128)S(1)} %get-tuple-element.18.pot_ref, s32[512,128]{1,0:T(8,128)S(1)} %get-tuple-element.19.bits_ref, s32[32,128]{1,0:T(8,128)} %get-tuple-element.20.block_hbm, ...), custom_call_target="tpu_custom_call" | custom-call | flops 20000000000 | bytes 60000000 | tf_op jit(solution)/shard_map/middle/pallas_call | solution.py:487
  42.9 0.0 collective-permute-done
  42.9 8.3 %all-to-all-start.1 = ((f32[64,1,1280]{2,1,0:T(1,128)}), f32[64,1,1280]{2,1,0:T(1,128)S(1)}, u32[]{:S(2)}, u32[]{:S(2)}) async-start(f32[64,1,1280]{2,1,0:T(1,128)} %bitcast.17), calls=%async_computation.1 | async-start | bytes 655360 | tf_op jit(solution)/shard_map/all_to_all | solution.py:471
  51.2 1.0 %add.6 = f32[2,2,64,256]{3,2,1,0:T(8,128)S(1)} add(f32[2,2,64,256]{3,2,1,0:T(8,128)S(1)} %get-tuple-element.15, f32[2,2,64,256]{3,2,1,0:T(8,128)} %collective-permute-done) | non-fusion elementwise | flops 65536 | bytes 786432 | tf_op jit(solution)/shard_map/add | solution.py:586
  52.2 3.4 %collective-permute-start.1 = (f32[2,64,256]{2,1,0:T(8,128)S(1)}, f32[2,64,256]{2,1,0:T(8,128)S(1)}, u32[]{:S(2)}, u32[]{:S(2)}) collective-permute-start(f32[2,64,256]{2,1,0:T(8,128)S(1)} %slice_bitcast_fusion), channel_id=1, source_target_pairs={{0,192},{64,128},{128,64},{192,0},{1,193},{65,129},{129,65},{193,1... | collective-permute-start | bytes 393224 | tf_op jit(solution)/shard_map/ppermute | solution.py:587
  55.6 6.1 %all-to-all-done.1 = f32[64,1,1280]{2,1,0:T(1,128)S(1)} async-done(((f32[64,1,1280]{2,1,0:T(1,128)}), f32[64,1,1280]{2,1,0:T(1,128)S(1)}, u32[]{:S(2)}, u32[]{:S(2)}) %all-to-all-start.1) | async-done | bytes 327712 | tf_op jit(solution)/shard_map/all_to_all | solution.py:471
  61.7 0.0 copy-done
  61.7 0.0 copy-done.1
  61.7 0.0 copy-done.2
  61.7 1.2 %after.1 = f32[2,64,256]{2,1,0:T(8,128)} custom-call(s32[32,128]{1,0:T(8,128)S(1)} %bitcast.16, f32[2,64,256]{2,1,0:T(8,128)S(1)} %copy-done.2, f32[640,128]{1,0:T(8,128)S(1)} %bitcast.13, bf16[256,1920]{1,0:T(8,128)(2,1)S(1)} %copy-done.1), custom_call_target="tpu_custom_call" | custom-call | flops 2000000000 | bytes 6000000 | tf_op jit(solution)/shard_map/after/pallas_call | solution.py:487
  62.9 0.0 collective-permute-done.1
  62.9 0.7 %fusion = f32[2,64,256]{2,1,0:T(8,128)} fusion(f32[2,64,256]{2,1,0:T(8,128)S(1)} %collective-permute-done.1, f32[2,2,64,256]{3,2,1,0:T(8,128)S(1)} %add.6), kind=kLoop, calls=%fused_computation.2 | loop fusion | flops 32768 | bytes 393216 | tf_op jit(solution)/shard_map/add | solution.py:598
  (1 shorter events, 0.0 us)
Async XLA Ops:
  3.2 20.8 %all-to-all-start = ((f32[64,1,1280]{2,1,0:T(1,128)}), f32[64,1,1280]{2,1,0:T(1,128)S(1)}, u32[]{:S(2)}, u32[]{:S(2)}) async-start(f32[64,1,1280]{2,1,0:T(1,128)} %bitcast.2), calls=%async_computation | async-start | bytes 655360 | tf_op jit(solution)/shard_map/all_to_all | solution.py:471
  19.9 23.1 %collective-permute-start = (f32[2,2,64,256]{3,2,1,0:T(8,128)S(1)}, f32[2,2,64,256]{3,2,1,0:T(8,128)}, u32[]{:S(2)}, u32[]{:S(2)}) collective-permute-start(f32[2,2,64,256]{3,2,1,0:T(8,128)S(1)} %get-tuple-element.21), channel_id=1, source_target_pairs={{0,64},{64,0},{128,192},{192,128},{1,65},{65,1},{129,193},{193,129... | collective-permute-start | bytes 786440 | tf_op jit(solution)/shard_map/ppermute | solution.py:583
  24.0 37.7 %copy-start = (s32[4096]{0:T(1024)S(1)}, s32[4096]{0:T(1024)}, u32[]{:S(2)}) copy-start(s32[4096]{0:T(1024)} %param.21) | copy-start | bytes 49156
  24.0 37.7 %copy-start.1 = (bf16[256,1920]{1,0:T(8,128)(2,1)S(1)}, bf16[256,1920]{1,0:T(8,128)(2,1)}, u32[]{:S(2)}) copy-start(bf16[256,1920]{1,0:T(8,128)(2,1)} %constant.31.clone.down_ref) | copy-start | bytes 2949124
  24.0 37.7 %copy-start.2 = (f32[2,64,256]{2,1,0:T(8,128)S(1)}, f32[2,64,256]{2,1,0:T(8,128)}, u32[]{:S(2)}) copy-start(f32[2,64,256]{2,1,0:T(8,128)} %get-tuple-element.14.corr_hbm.corr_ref) | copy-start | bytes 393220
  42.9 18.7 %all-to-all-start.1 = ((f32[64,1,1280]{2,1,0:T(1,128)}), f32[64,1,1280]{2,1,0:T(1,128)S(1)}, u32[]{:S(2)}, u32[]{:S(2)}) async-start(f32[64,1,1280]{2,1,0:T(1,128)} %bitcast.17), calls=%async_computation.1 | async-start | bytes 655360 | tf_op jit(solution)/shard_map/all_to_all | solution.py:471
  52.2 10.6 %collective-permute-start.1 = (f32[2,64,256]{2,1,0:T(8,128)S(1)}, f32[2,64,256]{2,1,0:T(8,128)S(1)}, u32[]{:S(2)}, u32[]{:S(2)}) collective-permute-start(f32[2,64,256]{2,1,0:T(8,128)S(1)} %slice_bitcast_fusion), channel_id=1, source_target_pairs={{0,192},{64,128},{128,64},{192,0},{1,193},{65,129},{129,65},{193,1... | collective-permute-start | bytes 393224 | tf_op jit(solution)/shard_map/ppermute | solution.py:587

commit v5 on v4

--- a/solution.py
+++ b/solution.py
@@ -452,7 +452,7 @@
         copy.wait()
 
 
-def after_kernel(map_ref, corr_ref, recv_ref, down_ref, out_ref):
+def after_kernel(map_ref, corr_ref, recv_ref, down_ref, mine_ref, last_ref, out_ref, next_ref):
     sticks = corr_ref.shape[1]
     kinetic = kinetic_of(map_ref, sticks)
     local = dot(down_ref[...], data_rows(recv_ref[...], 0))
@@ -460,6 +460,7 @@
     both = jnp.concatenate([kinetic, kinetic], 1)
     for b in range(BANDS):
         out_ref[b] = both * corr_ref[b] + local[b * sticks : (b + 1) * sticks]
+        next_ref[b] = mine_ref[b] + last_ref[b]
 
 
 def shape(*dims):
@@ -583,19 +584,17 @@
     came = lax.ppermute(passed, "bg", [(i, i ^ 1) for i in range(4)])
     product, came = lax.optimization_barrier((middle(place, received, local, bits, block, t), came))
     returned = exchange(product)
-    halved = kept + came
-    last = lax.ppermute(halved[1], "bg", [(i, 3 - i) for i in range(4)])
-    applied_correction = call(
+    last = lax.ppermute(kept[1] + came[1], "bg", [(i, 3 - i) for i in range(4)])
+    mine = kept[0] + came[0]
+    applied_correction, next_orbitals = call(
         after_kernel,
         "after",
         2,
-        (in_vmem(map_rows), in_vmem(correction), in_vmem(returned), in_vmem(t["stick_down"])),
-        shape(*orbitals.shape),
-        [VMEM] * 4,
-        VMEM,
-    )
-    applied_correction, last = lax.optimization_barrier((applied_correction, last))
-    next_orbitals = halved[0] + last
+        tuple(in_vmem(x) for x in (map_rows, correction, returned, t["stick_down"], mine, last)),
+        (shape(*orbitals.shape), shape(*orbitals.shape)),
+        [VMEM] * 6,
+        (VMEM, VMEM),
+    )
     return (next_orbitals, applied_correction)
 
 

time: 63.8 us -> 63.1 us (0.989)
  other arithmetic: 1.66 us -> 1 us
    all_to_all x2, waiting for transfers between devices: 6.98 us -> 1.06 us  [exchange(): lax.all_to_all(values, 'pw', 0, 0, tiled=True).reshape(GROUP * PARTS, 128)]
    ppermute x1, waiting for transfers between devices: 0.01 us -> 5.92 us  [on_device(): last = lax.ppermute(kept[1] + came[1], 'bg', [(i, 3 - i) for i in range(4)])]
    add x2 -> x1, other arithmetic: 1.66 us -> 1 us  [on_device(): last = lax.ppermute(kept[1] + came[1], 'bg', [(i, 3 - i) for i in range(4)])]
  transfers between devices with their start and end apart: 4 -> 4, of which waited for: 2 -> 3; matrix products, arithmetic and copies ran while one was open for 2% -> 2% of each run, Pallas kernels for 42% -> 40%
where the time goes in v5:
time: 63.1 us; the launch traced here: 62.8 us
  Pallas kernels  28.9 us (46%)
  starting transfers between devices  25.3 us (40%)
  waiting for transfers between devices  6.98 us (11%)
  other arithmetic  1 us (2%)
  between operations  0.69 us (1%)
    pallas_call x4, Pallas kernels, call(): pl.pallas_call(kernel, out_shape=out_shape, in_specs=in_specs, out_specs=...  28.9 us
    all_to_all x2, starting transfers between devices, exchange(): lax.all_to_all(values, 'pw', 0, 0, tiled=True).reshape(GROUP * PARTS, 128)  18.6 us
    ppermute x1, waiting for transfers between devices, on_device(): last = lax.ppermute(kept[1] + came[1], 'bg', [(i, 3 - i) for i in range(4)])  5.92 us
    ppermute x1, starting transfers between devices, on_device(): last = lax.ppermute(kept[1] + came[1], 'bg', [(i, 3 - i) for i in range(4)])  3.39 us
    ppermute x1, starting transfers between devices, on_device(): came = lax.ppermute(passed, 'bg', [(i, i ^ 1) for i in range(4)])  3.26 us
  transfers between devices with their start and end apart: 4, of which 3 were waited for; matrix products, arithmetic and copies ran while one was open for 2% of the time, Pallas kernels for 40%

profile of v5, /device:TPU:1, one launch (start us, length us, event | category | flops | bytes accessed | tf_op | source)
XLA Modules:
  0.0 62.8 jit_solution(7998529334545171569)
XLA Ops:
  0.6 2.5 %before.1 = (f32[640,128]{1,0:T(8,128)}, f32[2,64,256]{2,1,0:T(8,128)}) custom-call(f32[2]{0:T(128)} %values_hbm.1, s32[32,128]{1,0:T(8,128)} %bitcast.12, f32[2,64,256]{2,1,0:T(8,128)} %orb_hbm.3, f32[2,64,256]{2,1,0:T(8,128)} %app_hbm.1, bf16[640,512]{1,0:T(8,128)(2,1)} %constant.30.clone.up_hbm), custom_call_target="tpu_custom_call" | custom-call | flops 2000000000 | bytes 6000000 | tf_op jit(solution)/shard_map/before/pallas_call | solution.py:488
  3.2 10.4 %all-to-all-start = ((f32[64,1,1280]{2,1,0:T(1,128)}), f32[64,1,1280]{2,1,0:T(1,128)S(1)}, u32[]{:S(2)}, u32[]{:S(2)}) async-start(f32[64,1,1280]{2,1,0:T(1,128)} %bitcast.2), calls=%async_computation | async-start | bytes 655360 | tf_op jit(solution)/shard_map/all_to_all | solution.py:472
  13.5 6.3 %prepare.1 = (f32[5,256,256]{2,1,0:T(8,128)S(1)}, s32[512,128]{1,0:T(8,128)S(1)}, s32[32,128]{1,0:T(8,128)}, s32[32,128]{1,0:T(8,128)}, f32[2,2,64,256]{3,2,1,0:T(8,128)S(1)}, /*index=5*/f32[2,2,64,256]{3,2,1,0:T(8,128)S(1)}) custom-call(f32[8,16]{1,0:T(8,128)} %bitcast.16, s32[32,128]{1,0:T(8,128)} %bitcast.13, f32[2,64,256]{2,1,0:T(8,128)} %orb_hbm.3, ...), custom_call_target="tpu_custom_call" | custom-call | flops 7000000000 | bytes 21000000 | tf_op jit(solution)/shard_map/prepare/pallas_call | solution.py:488
  19.9 3.3 %collective-permute-start = (f32[2,2,64,256]{3,2,1,0:T(8,128)S(1)}, f32[2,2,64,256]{3,2,1,0:T(8,128)}, u32[]{:S(2)}, u32[]{:S(2)}) collective-permute-start(f32[2,2,64,256]{3,2,1,0:T(8,128)S(1)} %get-tuple-element.20), channel_id=1, source_target_pairs={{0,64},{64,0},{128,192},{192,128},{1,65},{65,1},{129,193},{193,129... | collective-permute-start | bytes 786440 | tf_op jit(solution)/shard_map/ppermute | solution.py:584
  23.1 0.9 %all-to-all-done = f32[64,1,1280]{2,1,0:T(1,128)S(1)} async-done(((f32[64,1,1280]{2,1,0:T(1,128)}), f32[64,1,1280]{2,1,0:T(1,128)S(1)}, u32[]{:S(2)}, u32[]{:S(2)}) %all-to-all-start) | async-done | bytes 327712 | tf_op jit(solution)/shard_map/all_to_all | solution.py:472
  24.0 0.0 copy-start
  24.0 0.0 copy-start.1
  24.0 0.0 copy-start.2
  24.0 18.9 %middle.1 = f32[640,128]{1,0:T(8,128)} custom-call(s32[32,128]{1,0:T(8,128)} %get-tuple-element.15.place_hbm, f32[640,128]{1,0:T(8,128)S(1)} %bitcast.10, f32[5,256,256]{2,1,0:T(8,128)S(1)} %get-tuple-element.17.pot_ref, s32[512,128]{1,0:T(8,128)S(1)} %get-tuple-element.18.bits_ref, s32[32,128]{1,0:T(8,128)} %get-tuple-element.19.block_hbm, ...), custom_call_target="tpu_custom_call" | custom-call | flops 20000000000 | bytes 60000000 | tf_op jit(solution)/shard_map/middle/pallas_call | solution.py:488
  42.9 0.0 collective-permute-done
  42.9 8.2 %all-to-all-start.1 = ((f32[64,1,1280]{2,1,0:T(1,128)}), f32[64,1,1280]{2,1,0:T(1,128)S(1)}, u32[]{:S(2)}, u32[]{:S(2)}) async-start(f32[64,1,1280]{2,1,0:T(1,128)} %bitcast.15), calls=%async_computation.1 | async-start | bytes 655360 | tf_op jit(solution)/shard_map/all_to_all | solution.py:472
  51.2 1.0 %add_bitcast_fusion = (f32[2,64,256]{2,1,0:T(8,128)S(1)}, f32[2,64,256]{2,1,0:T(8,128)S(1)}) fusion(f32[2,2,64,256]{3,2,1,0:T(8,128)} %collective-permute-done, f32[2,2,64,256]{3,2,1,0:T(8,128)S(1)} %get-tuple-element.22), kind=kLoop, calls=%fused_computation | loop fusion | flops 65536 | bytes 786432 | tf_op jit(solution)/shard_map/add | solution.py:587
  52.2 3.4 %collective-permute-start.1 = (f32[2,64,256]{2,1,0:T(8,128)S(1)}, f32[2,64,256]{2,1,0:T(8,128)S(1)}, u32[]{:S(2)}, u32[]{:S(2)}) collective-permute-start(f32[2,64,256]{2,1,0:T(8,128)S(1)} %get-tuple-element.26), channel_id=1, source_target_pairs={{0,192},{64,128},{128,64},{192,0},{1,193},{65,129},{129,65},{193,1... | collective-permute-start | bytes 393224 | tf_op jit(solution)/shard_map/ppermute | solution.py:587
  55.6 5.9 %collective-permute-done.1.last_ref = f32[2,64,256]{2,1,0:T(8,128)S(1)} collective-permute-done((f32[2,64,256]{2,1,0:T(8,128)S(1)}, f32[2,64,256]{2,1,0:T(8,128)S(1)}, u32[]{:S(2)}, u32[]{:S(2)}) %collective-permute-start.1) | collective-permute-done | bytes 131104 | tf_op jit(solution)/shard_map/ppermute | solution.py:587
  61.5 0.2 all-to-all-done.1
  61.7 0.0 copy-done
  61.7 0.0 copy-done.1
  61.7 0.0 copy-done.2
  61.7 1.2 %after.1 = (f32[2,64,256]{2,1,0:T(8,128)}, f32[2,64,256]{2,1,0:T(8,128)}) custom-call(s32[32,128]{1,0:T(8,128)S(1)} %bitcast.14, f32[2,64,256]{2,1,0:T(8,128)S(1)} %copy-done.2, f32[640,128]{1,0:T(8,128)S(1)} %bitcast.11, bf16[256,1920]{1,0:T(8,128)(2,1)S(1)} %copy-done.1, f32[2,64,256]{2,1,0:T(8,128)S(1)} %get-tuple-element.27.mine_ref, ...), custom_call_target="tpu_custom_call" | custom-call | flops 2000000000 | bytes 6000000 | tf_op jit(solution)/shard_map/after/pallas_call | solution.py:488
Async XLA Ops:
  3.2 20.8 %all-to-all-start = ((f32[64,1,1280]{2,1,0:T(1,128)}), f32[64,1,1280]{2,1,0:T(1,128)S(1)}, u32[]{:S(2)}, u32[]{:S(2)}) async-start(f32[64,1,1280]{2,1,0:T(1,128)} %bitcast.2), calls=%async_computation | async-start | bytes 655360 | tf_op jit(solution)/shard_map/all_to_all | solution.py:472
  19.9 23.1 %collective-permute-start = (f32[2,2,64,256]{3,2,1,0:T(8,128)S(1)}, f32[2,2,64,256]{3,2,1,0:T(8,128)}, u32[]{:S(2)}, u32[]{:S(2)}) collective-permute-start(f32[2,2,64,256]{3,2,1,0:T(8,128)S(1)} %get-tuple-element.20), channel_id=1, source_target_pairs={{0,64},{64,0},{128,192},{192,128},{1,65},{65,1},{129,193},{193,129... | collective-permute-start | bytes 786440 | tf_op jit(solution)/shard_map/ppermute | solution.py:584
  24.0 37.6 %copy-start = (s32[4096]{0:T(1024)S(1)}, s32[4096]{0:T(1024)}, u32[]{:S(2)}) copy-start(s32[4096]{0:T(1024)} %param.21) | copy-start | bytes 49156
  24.0 37.6 %copy-start.1 = (bf16[256,1920]{1,0:T(8,128)(2,1)S(1)}, bf16[256,1920]{1,0:T(8,128)(2,1)}, u32[]{:S(2)}) copy-start(bf16[256,1920]{1,0:T(8,128)(2,1)} %constant.31.clone.down_ref) | copy-start | bytes 2949124
  24.0 37.7 %copy-start.2 = (f32[2,64,256]{2,1,0:T(8,128)S(1)}, f32[2,64,256]{2,1,0:T(8,128)}, u32[]{:S(2)}) copy-start(f32[2,64,256]{2,1,0:T(8,128)} %get-tuple-element.14.corr_hbm.corr_ref) | copy-start | bytes 393220
  42.9 18.7 %all-to-all-start.1 = ((f32[64,1,1280]{2,1,0:T(1,128)}), f32[64,1,1280]{2,1,0:T(1,128)S(1)}, u32[]{:S(2)}, u32[]{:S(2)}) async-start(f32[64,1,1280]{2,1,0:T(1,128)} %bitcast.15), calls=%async_computation.1 | async-start | bytes 655360 | tf_op jit(solution)/shard_map/all_to_all | solution.py:472
  52.2 9.3 %collective-permute-start.1 = (f32[2,64,256]{2,1,0:T(8,128)S(1)}, f32[2,64,256]{2,1,0:T(8,128)S(1)}, u32[]{:S(2)}, u32[]{:S(2)}) collective-permute-start(f32[2,64,256]{2,1,0:T(8,128)S(1)} %get-tuple-element.26), channel_id=1, source_target_pairs={{0,192},{64,128},{128,64},{192,0},{1,193},{65,129},{129,65},{193,1... | collective-permute-start | bytes 393224 | tf_op jit(solution)/shard_map/ppermute | solution.py:587

commit v6 on v5

--- a/solution.py
+++ b/solution.py
@@ -540,7 +540,7 @@
             pltpu.HBM(map_rows.shape, jnp.int32),
             pltpu.HBM(map_rows.shape, jnp.int32),
             pltpu.VMEM((2, BANDS, sticks, doubled), F32),
-            pltpu.VMEM((2, BANDS, sticks, doubled), F32),
+            pltpu.HBM((2, BANDS, sticks, doubled), F32),
         ),
         [ANY] * 7,
         (VMEM,) * 6,

time: 63.1 us -> 63.2 us (level)
  other arithmetic: 1 us -> 0.04 us
  waiting for transfers between devices: 6.98 us -> 7.87 us
    add x1, other arithmetic: 1 us -> 0.04 us  [on_device(): last = lax.ppermute(kept[1] + came[1], 'bg', [(i, 3 - i) for i in range(4)])]
    ppermute x1, waiting for transfers between devices: 5.92 us -> 6.84 us  [on_device(): last = lax.ppermute(kept[1] + came[1], 'bg', [(i, 3 - i) for i in range(4)])]
  transfers between devices with their start and end apart: 4 -> 4, of which waited for: 3 -> 3; matrix products, arithmetic and copies ran while one was open for 2% -> 0% of each run, Pallas kernels for 40% -> 40%
where the time goes in v6:
time: 63.2 us; the launch traced here: 62.9 us
  Pallas kernels  29 us (46%)
  starting transfers between devices  25.3 us (40%)
  waiting for transfers between devices  7.87 us (12%)
  between operations  0.69 us (1%)
    pallas_call x4, Pallas kernels, call(): pl.pallas_call(kernel, out_shape=out_shape, in_specs=in_specs, out_specs=...  29 us
    all_to_all x2, starting transfers between devices, exchange(): lax.all_to_all(values, 'pw', 0, 0, tiled=True).reshape(GROUP * PARTS, 128)  18.7 us
    ppermute x1, waiting for transfers between devices, on_device(): last = lax.ppermute(kept[1] + came[1], 'bg', [(i, 3 - i) for i in range(4)])  6.84 us
    ppermute x1, starting transfers between devices, on_device(): last = lax.ppermute(kept[1] + came[1], 'bg', [(i, 3 - i) for i in range(4)])  3.39 us
    ppermute x1, starting transfers between devices, on_device(): came = lax.ppermute(passed, 'bg', [(i, i ^ 1) for i in range(4)])  3.26 us
  transfers between devices with their start and end apart: 4, of which 3 were waited for; matrix products, arithmetic and copies ran while one was open for 0% of the time, Pallas kernels for 40%

profile of v6, /device:TPU:1, one launch (start us, length us, event | category | flops | bytes accessed | tf_op | source)
XLA Modules:
  0.0 62.9 jit_solution(257034750139677238)
XLA Ops:
  0.6 2.5 %before.1 = (f32[640,128]{1,0:T(8,128)}, f32[2,64,256]{2,1,0:T(8,128)}) custom-call(f32[2]{0:T(128)} %values_hbm.1, s32[32,128]{1,0:T(8,128)} %bitcast.12, f32[2,64,256]{2,1,0:T(8,128)} %orb_hbm.3, f32[2,64,256]{2,1,0:T(8,128)} %app_hbm.1, bf16[640,512]{1,0:T(8,128)(2,1)} %constant.30.clone.up_hbm), custom_call_target="tpu_custom_call" | custom-call | flops 2000000000 | bytes 6000000 | tf_op jit(solution)/shard_map/before/pallas_call | solution.py:488
  3.2 10.4 %all-to-all-start = ((f32[64,1,1280]{2,1,0:T(1,128)}), f32[64,1,1280]{2,1,0:T(1,128)S(1)}, u32[]{:S(2)}, u32[]{:S(2)}) async-start(f32[64,1,1280]{2,1,0:T(1,128)} %bitcast.2), calls=%async_computation | async-start | bytes 655360 | tf_op jit(solution)/shard_map/all_to_all | solution.py:472
  13.5 6.4 %prepare.1 = (f32[5,256,256]{2,1,0:T(8,128)S(1)}, s32[512,128]{1,0:T(8,128)S(1)}, s32[32,128]{1,0:T(8,128)}, s32[32,128]{1,0:T(8,128)}, f32[2,2,64,256]{3,2,1,0:T(8,128)S(1)}, /*index=5*/f32[2,2,64,256]{3,2,1,0:T(8,128)}) custom-call(f32[8,16]{1,0:T(8,128)} %bitcast.16, s32[32,128]{1,0:T(8,128)} %bitcast.13, f32[2,64,256]{2,1,0:T(8,128)} %orb_hbm.3, ...), custom_call_target="tpu_custom_call" | custom-call | flops 7000000000 | bytes 21000000 | tf_op jit(solution)/shard_map/prepare/pallas_call | solution.py:488
  19.9 3.3 %collective-permute-start = (f32[2,2,64,256]{3,2,1,0:T(8,128)}, f32[2,2,64,256]{3,2,1,0:T(8,128)S(1)}, u32[]{:S(2)}, u32[]{:S(2)}) collective-permute-start(f32[2,2,64,256]{3,2,1,0:T(8,128)} %get-tuple-element.20), channel_id=1, source_target_pairs={{0,64},{64,0},{128,192},{192,128},{1,65},{65,1},{129,193},{193,129... | collective-permute-start | bytes 786440 | tf_op jit(solution)/shard_map/ppermute | solution.py:584
  23.2 0.8 %all-to-all-done = f32[64,1,1280]{2,1,0:T(1,128)S(1)} async-done(((f32[64,1,1280]{2,1,0:T(1,128)}), f32[64,1,1280]{2,1,0:T(1,128)S(1)}, u32[]{:S(2)}, u32[]{:S(2)}) %all-to-all-start) | async-done | bytes 327712 | tf_op jit(solution)/shard_map/all_to_all | solution.py:472
  24.0 0.0 copy-start
  24.0 0.0 copy-start.1
  24.0 0.0 copy-start.2
  24.0 18.9 %middle.1 = f32[640,128]{1,0:T(8,128)} custom-call(s32[32,128]{1,0:T(8,128)} %get-tuple-element.15.place_hbm, f32[640,128]{1,0:T(8,128)S(1)} %bitcast.10, f32[5,256,256]{2,1,0:T(8,128)S(1)} %get-tuple-element.17.pot_ref, s32[512,128]{1,0:T(8,128)S(1)} %get-tuple-element.18.bits_ref, s32[32,128]{1,0:T(8,128)} %get-tuple-element.19.block_hbm, ...), custom_call_target="tpu_custom_call" | custom-call | flops 20000000000 | bytes 60000000 | tf_op jit(solution)/shard_map/middle/pallas_call | solution.py:488
  42.9 0.0 collective-permute-done
  42.9 8.3 %all-to-all-start.1 = ((f32[64,1,1280]{2,1,0:T(1,128)}), f32[64,1,1280]{2,1,0:T(1,128)S(1)}, u32[]{:S(2)}, u32[]{:S(2)}) async-start(f32[64,1,1280]{2,1,0:T(1,128)} %bitcast.15), calls=%async_computation.1 | async-start | bytes 655360 | tf_op jit(solution)/shard_map/all_to_all | solution.py:472
  51.3 3.4 %collective-permute-start.1 = (f32[2,64,256]{2,1,0:T(8,128)S(1)}, f32[2,64,256]{2,1,0:T(8,128)S(1)}, u32[]{:S(2)}, u32[]{:S(2)}) collective-permute-start(f32[2,64,256]{2,1,0:T(8,128)S(1)} %get-tuple-element.26), channel_id=1, source_target_pairs={{0,192},{64,128},{128,64},{192,0},{1,193},{65,129},{129,65},{193,1... | collective-permute-start | bytes 393224 | tf_op jit(solution)/shard_map/ppermute | solution.py:587
  54.7 6.8 %collective-permute-done.1.last_ref = f32[2,64,256]{2,1,0:T(8,128)S(1)} collective-permute-done((f32[2,64,256]{2,1,0:T(8,128)S(1)}, f32[2,64,256]{2,1,0:T(8,128)S(1)}, u32[]{:S(2)}, u32[]{:S(2)}) %collective-permute-start.1) | collective-permute-done | bytes 131104 | tf_op jit(solution)/shard_map/ppermute | solution.py:587
  61.5 0.2 all-to-all-done.1
  61.7 0.0 copy-done
  61.7 0.0 copy-done.1
  61.7 0.0 copy-done.2
  61.7 1.2 %after.1 = (f32[2,64,256]{2,1,0:T(8,128)}, f32[2,64,256]{2,1,0:T(8,128)}) custom-call(s32[32,128]{1,0:T(8,128)S(1)} %bitcast.14, f32[2,64,256]{2,1,0:T(8,128)S(1)} %copy-done.2, f32[640,128]{1,0:T(8,128)S(1)} %bitcast.11, bf16[256,1920]{1,0:T(8,128)(2,1)S(1)} %copy-done.1, f32[2,64,256]{2,1,0:T(8,128)S(1)} %get-tuple-element.27.mine_ref, ...), custom_call_target="tpu_custom_call" | custom-call | flops 2000000000 | bytes 6000000 | tf_op jit(solution)/shard_map/after/pallas_call | solution.py:488
  (1 shorter events, 0.0 us)
Async XLA Ops:
  3.2 20.8 %all-to-all-start = ((f32[64,1,1280]{2,1,0:T(1,128)}), f32[64,1,1280]{2,1,0:T(1,128)S(1)}, u32[]{:S(2)}, u32[]{:S(2)}) async-start(f32[64,1,1280]{2,1,0:T(1,128)} %bitcast.2), calls=%async_computation | async-start | bytes 655360 | tf_op jit(solution)/shard_map/all_to_all | solution.py:472
  19.9 23.0 %collective-permute-start = (f32[2,2,64,256]{3,2,1,0:T(8,128)}, f32[2,2,64,256]{3,2,1,0:T(8,128)S(1)}, u32[]{:S(2)}, u32[]{:S(2)}) collective-permute-start(f32[2,2,64,256]{3,2,1,0:T(8,128)} %get-tuple-element.20), channel_id=1, source_target_pairs={{0,64},{64,0},{128,192},{192,128},{1,65},{65,1},{129,193},{193,129... | collective-permute-start | bytes 786440 | tf_op jit(solution)/shard_map/ppermute | solution.py:584
  24.0 37.7 %copy-start = (s32[4096]{0:T(1024)S(1)}, s32[4096]{0:T(1024)}, u32[]{:S(2)}) copy-start(s32[4096]{0:T(1024)} %param.21) | copy-start | bytes 49156
  24.0 37.7 %copy-start.1 = (bf16[256,1920]{1,0:T(8,128)(2,1)S(1)}, bf16[256,1920]{1,0:T(8,128)(2,1)}, u32[]{:S(2)}) copy-start(bf16[256,1920]{1,0:T(8,128)(2,1)} %constant.31.clone.down_ref) | copy-start | bytes 2949124
  24.0 37.7 %copy-start.2 = (f32[2,64,256]{2,1,0:T(8,128)S(1)}, f32[2,64,256]{2,1,0:T(8,128)}, u32[]{:S(2)}) copy-start(f32[2,64,256]{2,1,0:T(8,128)} %get-tuple-element.14.corr_hbm.corr_ref) | copy-start | bytes 393220
  42.9 18.8 %all-to-all-start.1 = ((f32[64,1,1280]{2,1,0:T(1,128)}), f32[64,1,1280]{2,1,0:T(1,128)S(1)}, u32[]{:S(2)}, u32[]{:S(2)}) async-start(f32[64,1,1280]{2,1,0:T(1,128)} %bitcast.15), calls=%async_computation.1 | async-start | bytes 655360 | tf_op jit(solution)/shard_map/all_to_all | solution.py:472
  51.3 10.2 %collective-permute-start.1 = (f32[2,64,256]{2,1,0:T(8,128)S(1)}, f32[2,64,256]{2,1,0:T(8,128)S(1)}, u32[]{:S(2)}, u32[]{:S(2)}) collective-permute-start(f32[2,64,256]{2,1,0:T(8,128)S(1)} %get-tuple-element.26), channel_id=1, source_target_pairs={{0,192},{64,128},{128,64},{192,0},{1,193},{65,129},{129,65},{193,1... | collective-permute-start | bytes 393224 | tf_op jit(solution)/shard_map/ppermute | solution.py:587
